TPU v7x, 128 devices: a whole 4x4x4 slice. The times are simulated.
128 devices in a mesh: src: 16 (over z, y), tgt: 8 (over x, core).
Axes of the slice: x: 4, y: 4, z: 4, core: 2. Of those that a mesh axis runs over, the one named last changes fastest.
Arguments:
- src_points: float32 [3, 2097152], P(None, ('src', 'tgt'))
- tgt_points: float32 [3, 2097152], P(None, ('src', 'tgt'))
- src_count: int32 [8192], P(('src', 'tgt')), may hold values from 128 to 256
- tgt_count: int32 [8192], P(('src', 'tgt')), may hold values from 128 to 256
- pair_list: int32 [2, 40960], P(None, ('src', 'tgt')), may hold values from 0 to 67, as said below
- pair_total: int32 [128], P(('src', 'tgt')), may hold values from 1 to 320, as said below
- rhs: float32 [8, 2097152], P(None, ('src', 'tgt'))
Outputs:
- coefficients: float32 [8, 2097152], P(None, ('src', 'tgt'))
- mapped: float32 [8, 2097152], P(None, ('src', 'tgt'))
Inputs may be any that keep to these rules, and one draw needn't show every extreme that they name: `pair_list`: pair (a, b) in a device's numbering has a among its own 64 blocks and 0 <= b - a <= 4, where b >= 64 names block b - 64 of the next device. Every pair of blocks in which a source or target point lies within distance 4 of a source point of the other is listed exactly once, by the device that holds the lower block; listed pairs may also include blocks with no such points. Slots from pair_total on hold (0, 0). `pair_total`: some device has all 320 slots live in every draw.
All inputs are finite; a program needn't handle non-finite values.
Results may differ from a plain program's by a relative error of at most 0.0003.
Values sent between devices are 32-bit elements; how exact they have to be, the bound alone decides.
A program may use at most 64 MiB of HBM per device.

v0:
```python
import jax
import jax.numpy as jnp
from jax import lax
from jax.sharding import PartitionSpec as P

R = 4
ITERS = 2


group_size = 8


def from_behind(x, axis, by):
    peers = lax.axis_size(axis)
    pairs = [(i, i + by) for i in range(peers) if 0 <= i + by < peers]
    return lax.ppermute(x, axis, pairs)


def wendland(left, right, left_mask, right_mask):
    offset = left[:, 0, :, None] - right[:, 0, None, :]
    distance = offset * offset
    for axis_number in (1, 2):
        offset = left[:, axis_number, :, None] - right[:, axis_number, None, :]
        distance = distance + offset * offset
    scaled = jnp.sqrt(distance) * (1.0 / R)
    remain = jnp.maximum(1.0 - scaled, 0.0)
    squared = remain * remain
    return squared * squared * (5.0 - 4.0 * remain) * left_mask[:, :, None] * right_mask[:, None, :]


def squares(residual):
    return lax.psum(jnp.sum(residual * residual, axis=(1, 2)), ("src", "tgt"))


def on_device(src_points, tgt_points, src_count, tgt_count, pair_list, pair_total, rhs):
    blocks = src_count.shape[0]
    width = src_points.shape[1] // blocks
    fields = rhs.shape[0]
    highest = lax.Precision.HIGHEST
    slots = jnp.arange(width)
    source_mask = (slots[None, :] < src_count[:, None]).astype(jnp.float32)
    target_mask = (slots[None, :] < tgt_count[:, None]).astype(jnp.float32)
    geometry = jnp.concatenate(
        [
            src_points.reshape(3, blocks, width),
            tgt_points.reshape(3, blocks, width),
            source_mask[None],
            target_mask[None],
        ],
        0,
    )
    capacity = pair_list.shape[1]
    padded = -(-capacity // group_size) * group_size
    beside = from_behind(geometry[:, :R], ("src", "tgt"), -1)
    extended = jnp.concatenate([geometry, beside], 1)
    first = pair_list[0]
    second = pair_list[1]
    live = (jnp.arange(padded) < pair_total[0]).astype(jnp.float32)
    first, second, live = (first, second, live)
    segments = [(first, second, live, live * (first != second).astype(jnp.float32), pair_total[0])]

    def spread(values, group_fn):
        following = from_behind(values[:, :R], ("src", "tgt"), -1)
        acc = run_pairs(jnp.concatenate([values, following], 1), group_fn)
        returned = from_behind(acc[:, blocks:], ("src", "tgt"), 1)
        return acc[:, :blocks] + jnp.pad(returned, ((0, 0), (0, blocks - R), (0, 0)))

    points_source = extended[0:3].transpose(1, 0, 2)
    points_target = extended[3:6].transpose(1, 0, 2)
    mask_source = extended[6]
    mask_target = extended[7]

    def run_pairs(values, group_fn):
        acc = jnp.zeros((fields, values.shape[1], width), jnp.float32)
        first_idx, second_idx, weight_f, weight_b, count = segments[0]
        groups = (count + group_size - 1) // group_size

        def loop_body(
            index,
            acc,
            first_idx=first_idx,
            second_idx=second_idx,
            weight_f=weight_f,
            weight_b=weight_b,
        ):
            start = index * group_size
            lower = lax.dynamic_slice_in_dim(first_idx, start, group_size)
            upper = lax.dynamic_slice_in_dim(second_idx, start, group_size)
            ahead_w = lax.dynamic_slice_in_dim(weight_f, start, group_size)
            behind_w = lax.dynamic_slice_in_dim(weight_b, start, group_size)
            return group_fn(acc, lower, upper, ahead_w, behind_w, values)

        acc = lax.fori_loop(0, groups, loop_body, acc)
        return acc

    def operator_group(acc, lower, upper, ahead_w, behind_w, values):
        kernel = wendland(
            points_source[lower], points_source[upper], mask_source[lower], mask_source[upper]
        )
        ahead = (
            jnp.einsum("gij,fgj->fgi", kernel, values[:, upper], precision=highest)
            * ahead_w[None, :, None]
        )
        behind = (
            jnp.einsum("gij,fgi->fgj", kernel, values[:, lower], precision=highest)
            * behind_w[None, :, None]
        )
        return acc.at[:, lower].add(ahead).at[:, upper].add(behind)

    def evaluation_group(acc, lower, upper, ahead_w, behind_w, values):
        kernel_f = wendland(
            points_target[lower], points_source[upper], mask_target[lower], mask_source[upper]
        )
        kernel_b = wendland(
            points_target[upper], points_source[lower], mask_target[upper], mask_source[lower]
        )
        ahead = (
            jnp.einsum("gij,fgj->fgi", kernel_f, values[:, upper], precision=highest)
            * ahead_w[None, :, None]
        )
        behind = (
            jnp.einsum("gij,fgj->fgi", kernel_b, values[:, lower], precision=highest)
            * behind_w[None, :, None]
        )
        return acc.at[:, lower].add(ahead).at[:, upper].add(behind)

    field = rhs.reshape(fields, blocks, width) * source_mask[None]
    solution = jnp.zeros_like(field)
    residual = field
    direction = field
    norm_now = squares(residual)
    for step in range(ITERS):
        image = spread(direction, operator_group)
        alpha = norm_now / lax.psum(jnp.sum(direction * image, axis=(1, 2)), ("src", "tgt"))
        solution = solution + alpha[:, None, None] * direction
        residual = residual - alpha[:, None, None] * image
        if step + 1 < ITERS:
            norm_next = squares(residual)
            direction = residual + (norm_next / norm_now)[:, None, None] * direction
            norm_now = norm_next
    mapped = spread(solution, evaluation_group)
    return (solution.reshape(fields, blocks * width), mapped.reshape(fields, blocks * width))


def solution(mesh):
    return jax.shard_map(
        on_device,
        mesh=mesh,
        in_specs=(
            P(None, ("src", "tgt")),
            P(None, ("src", "tgt")),
            P(("src", "tgt")),
            P(("src", "tgt")),
            P(None, ("src", "tgt")),
            P(("src", "tgt")),
            P(None, ("src", "tgt")),
        ),
        out_specs=(P(None, ("src", "tgt")), P(None, ("src", "tgt"))),
        check_vma=False,
    )
```

profile of v0, /device:TPU:96, one launch (start us, length us, event | category | flops | bytes accessed | tf_op | source)
XLA Modules:
  0.0 2048.4 jit_solution(15491672637451060360)
XLA Ops:
  3.3 6.4 collective-permute-start.1
  14.2 563.9 %while.30 = (s32[]{:T(128)}, f32[8,68,256]{2,0,1:T(8,128)S(1)}, s32[]{:T(128)}, s32[320]{0:T(512)S(1)}, s32[320]{0:T(512)S(1)}, /*index=5*/f32[8,68,256]{2,0,1:T...) while((s32[]{:T(128)}, f32[8,68,256]{2,0,1:T(8,128)S(1)}, ...), condition=%wide.region_5.6_spmd, body=%wide.region_2.5_spmd.sunk | while | flops 119605296 | bytes 1385279 | solution.py:93
  45.5 4.5 convolution_multiply_fusion.8
  59.6 4.5 convolution_multiply_fusion.8
  73.7 4.5 convolution_multiply_fusion.8
  87.8 4.5 convolution_multiply_fusion.8
  101.9 4.5 convolution_multiply_fusion.8
  116.0 4.5 convolution_multiply_fusion.8
  130.1 4.5 convolution_multiply_fusion.8
  158.3 4.5 convolution_multiply_fusion.8
  172.4 4.5 convolution_multiply_fusion.8
  186.5 4.5 convolution_multiply_fusion.8
  200.6 4.5 convolution_multiply_fusion.8
  214.7 4.5 convolution_multiply_fusion.8
  285.2 4.5 convolution_multiply_fusion.8
  299.3 4.5 convolution_multiply_fusion.8
  580.3 7.3 collective-permute-done.2
  587.8 62.3 %all-reduce.3 = (f32[8]{0:T(128)S(1)}, f32[8]{0:T(128)S(1)}) all-reduce(f32[8]{0:T(128)S(1)} %multiply_reduce_fusion.3, f32[8]{0:T(128)S(1)} %multiply_reduce_fusion.2), channel_id=1, replica_groups=mesh['src'=16,'tgt'=8] {'src','tgt'}, use_global_device_ids=true, to_apply=%region_1.0 | all-reduce | flops 16 | bytes 128 | tf_op jit(solution)/shard_map/psum | solution.py:32
  650.6 62.2 %psum.30 = f32[8]{0:T(128)S(1)} all-reduce(f32[8]{0:T(128)S(1)} %multiply_reduce_fusion.1), channel_id=1, replica_groups=mesh['src'=16,'tgt'=8] {'src','tgt'}, use_global_device_ids=true, to_apply=%region_9.10 | all-reduce | flops 8 | bytes 64 | tf_op jit(solution)/shard_map/psum | solution.py:32
  718.9 563.9 %while.31 = (s32[]{:T(128)}, f32[8,68,256]{2,0,1:T(8,128)S(1)}, s32[]{:T(128)}, s32[320]{0:T(512)S(1)}, s32[320]{0:T(512)S(1)}, /*index=5*/f32[8,68,256]{2,0,1:T...) while((s32[]{:T(128)}, f32[8,68,256]{2,0,1:T(8,128)S(1)}, ...), condition=%wide.region_13.14_spmd, body=%wide.region_10.13_spmd.sunk | while | flops 119605296 | bytes 1385279 | solution.py:93
  1284.8 7.5 collective-permute-done.4
  1292.5 62.3 %psum.31 = f32[8]{0:T(128)S(1)} all-reduce(f32[8]{0:T(128)S(1)} %multiply_reduce_fusion), channel_id=1, replica_groups=mesh['src'=16,'tgt'=8] {'src','tgt'}, use_global_device_ids=true, to_apply=%region_15.16 | all-reduce | flops 8 | bytes 64 | tf_op jit(solution)/shard_map/psum | solution.py:134
  1359.3 678.8 %while.32 = (s32[]{:T(128)}, f32[8,68,256]{2,0,1:T(8,128)S(1)}, s32[]{:T(128)}, s32[320]{0:T(512)S(1)}, s32[320]{0:T(512)S(1)}, /*index=5*/f32[8,68,256]{2,0,1:T...) while((s32[]{:T(128)}, f32[8,68,256]{2,0,1:T(8,128)S(1)}, ...), condition=%wide.region_19.20_spmd, body=%wide.region_16.19_spmd.sunk | while | flops 119605296 | bytes 1713103 | solution.py:93
  2040.0 7.5 collective-permute-done.6
  (3284 shorter events, 1748.4 us)
Async XLA Ops:
  2.1 7.6 copy-start.2
  2.1 7.7 copy-start
  3.3 10.1 collective-permute-start.1
  9.8 3.4 copy-start.3
  9.9 4.2 collective-permute-start
  578.1 9.5 collective-permute-start.2
  713.1 5.7 collective-permute-start.3
  1282.8 9.5 collective-permute-start.4
  1355.1 4.2 copy-start.1
  1355.1 4.1 collective-permute-start.5
  2038.1 9.5 collective-permute-start.6
where the time goes:
time: 2050 us
  matrix products  1050 us (51%)
  local copies, waits for them, and re-layouts  527 us (26%)
  other arithmetic  219 us (11%)
  blocking collectives  187 us (9%)
  waiting for transfers between devices  25.7 us (1%)
  starting transfers between devices  21.4 us (1%)
    dot_general x80, matrix products, operator_group(): jnp.einsum('gij,fgj->fgi', kernel, values[:, upper], precision=highest)  361 us
    dot_general x80, matrix products, operator_group(): jnp.einsum('gij,fgi->fgj', kernel, values[:, lower], precision=highest)  325 us
    dot_general x40, matrix products, evaluation_group(): jnp.einsum('gij,fgj->fgi', kernel_f, values[:, upper], precision=highest)  180 us
    dot_general x40, matrix products, evaluation_group(): jnp.einsum('gij,fgj->fgi', kernel_b, values[:, lower], precision=highest)  180 us
    scatter-add x160, other arithmetic, operator_group(): return acc.at[:, lower].add(ahead).at[:, upper].add(behind)  135 us
    psum x2, blocking collectives, squares(): return lax.psum(jnp.sum(residual * residual, axis=(1, 2)), ('src', 'tgt'))  125 us
    scatter-add x80, other arithmetic, evaluation_group(): return acc.at[:, lower].add(ahead).at[:, upper].add(behind)  68.4 us
    psum x1, blocking collectives, on_device(): lax.psum(jnp.sum(direction * image, axis=(1, 2)), ('src', 'tgt'))  62.3 us
  transfers between devices with their start and end apart: 7, of which 6 were waited for; matrix products, arithmetic and copies ran while one was open for 0% of the time, Pallas kernels for 0%

commit v1 on v0

v1 whole, which is shorter than its diff:
```python
import functools

import jax
import jax.numpy as jnp
from jax import lax
from jax.experimental import pallas as pl
from jax.experimental.pallas import tpu as pltpu
from jax.sharding import PartitionSpec as P

R = 4
BP = 256
F = 8
GS = R * BP
HALO = 2
LANES = 128
CHUNKS = GS // LANES
BINS = 128
WIN = 192
ROW_STRIDE = GS + WIN
VAL_STRIDE = GS + 384
SEG = 256
AXES = ("src", "tgt")
f32 = jnp.float32
bf16 = jnp.bfloat16
i32 = jnp.int32


def iota(shape, dim):
    return lax.broadcasted_iota(i32, shape, dim)


def dot(a, b, dims=((1,), (0,))):
    return lax.dot_general(a, b, (dims, ((), ())), preferred_element_type=f32)


def slot_mask(cnt_ref, group):
    slot = iota((1, GS), 1)
    block = slot // BP
    limit = jnp.zeros((1, GS), i32)
    for k in range(R):
        limit = jnp.where(block == k, cnt_ref[group * R + k], limit)
    return (slot % BP) < limit


def live_total(cnt_ref, group):
    total = cnt_ref[group * R]
    for k in range(1, R):
        total = total + cnt_ref[group * R + k]
    return total


def order(y, live):
    low = jnp.min(jnp.where(live, y, jnp.inf))
    high = jnp.max(jnp.where(live, y, -jnp.inf))
    scale = BINS / jnp.maximum(high - low, 1e-30)
    scaled = jnp.minimum(jnp.maximum((y - low) * scale, 0.0), BINS - 1.0)
    bin_of = jnp.where(live, scaled.astype(i32), BINS)
    ones_col = iota((SEG, SEG + LANES), 1)
    upper = ((iota((SEG, SEG + LANES), 0) < ones_col) | (ones_col >= SEG)).astype(f32).astype(bf16)
    lower = (iota((BINS, BINS), 1) < iota((BINS, BINS), 0)).astype(f32).astype(bf16)
    base = jnp.zeros((BINS, LANES), f32)
    members, counts, totals = [], [], []
    for s in range(GS // SEG):
        member = (bin_of[:, s * SEG:(s + 1) * SEG] == iota((BINS, SEG), 0)).astype(f32)
        both = dot(member.astype(bf16), upper)
        members.append(member)
        counts.append(both[:, :SEG])
        totals.append(both[:, SEG:])
        base = base + dot(lower, both[:, SEG:].astype(bf16))
    places = []
    for s in range(GS // SEG):
        offset = jnp.concatenate([base] * (SEG // LANES), 1)
        places.append(jnp.sum(members[s] * (counts[s] + offset), axis=0, keepdims=True))
        base = base + totals[s]
    place = jnp.concatenate(places, 1).astype(i32)
    slot = iota((1, GS), 1)
    row = iota((16, GS), 0)
    digit = jnp.where(row < 8, slot // 32, slot % 32).astype(f32)
    left = jnp.where((place // LANES) == (row % 8), digit, 0.0).astype(bf16)
    within = jnp.where(live, place % LANES, -1)
    right = (within == iota((LANES, GS), 0)).astype(f32).astype(bf16)
    both = dot(left, right, ((1,), (1,)))
    slots = (both[:8] * 32.0 + both[8:]).astype(i32)
    return place, slots


def gather(values, index):
    index = jnp.broadcast_to(index, (8, LANES))
    lane = index % LANES
    tile = index // LANES
    out = jnp.take_along_axis(values[:, :LANES], lane, axis=1)
    for k in range(1, CHUNKS):
        part = jnp.take_along_axis(values[:, k * LANES:(k + 1) * LANES], lane, axis=1)
        out = jnp.where(tile == k, part, out)
    return out


def split(v):
    high = v.astype(bf16)
    return high, (v - high.astype(f32)).astype(bf16)


def local_kernel(
    me_ref, scnt_ref, tcnt_ref, src_ref, tgt_ref,
    splace_ref, tplace_ref, w1_ref, mf_ref, mw_ref, sums_ref,
    rows_ref, vf_ref, vw_ref, lane_ref, tlane_ref, w2_ref, wins_v, wins_s, sem,
):
    own = tgt_ref.shape[1] // GS
    total = own + 2 * HALO

    def clear(g, _):
        rows_ref[pl.ds(pl.multiple_of(g * ROW_STRIDE + GS, 8), WIN), :] = jnp.zeros((WIN, LANES), f32)
        vf_ref[:, pl.ds(pl.multiple_of(g * VAL_STRIDE + GS, LANES), 384)] = jnp.zeros((F, 384), f32)
        vw_ref[:, pl.ds(pl.multiple_of(g * VAL_STRIDE + GS, LANES), 384)] = jnp.zeros((F, 384), f32)
        return 0

    lax.fori_loop(0, total, clear, 0)

    def sort_source(g, _):
        at = pl.multiple_of(g * GS, GS)
        live = slot_mask(scnt_ref, g)
        count = live_total(scnt_ref, g)
        points = src_ref[8:16, pl.ds(at, GS)]
        field = src_ref[0:8, pl.ds(at, GS)]
        place, slots = order(points[1:2], live)
        splace_ref[:, pl.ds(at, GS)] = place
        for h in range(CHUNKS):
            index = slots[h:h + 1]
            here = (iota((8, LANES), 1) + h * LANES) < count
            moved = gather(points, index)
            lane_ref[:, pl.ds(at + h * LANES, LANES)] = moved
            wide = jnp.concatenate([moved, jnp.zeros((LANES - 8, LANES), f32)], 0)
            rows_ref[pl.ds(pl.multiple_of(g * ROW_STRIDE + h * LANES, 8), LANES), :] = wide.T
            vf_ref[:, pl.ds(pl.multiple_of(g * VAL_STRIDE + h * LANES, LANES), LANES)] = jnp.where(
                here, gather(field, index), 0.0
            )
        return 0

    lax.fori_loop(0, total, sort_source, 0)

    def sort_target(g, _):
        at = pl.multiple_of(g * GS, GS)
        live = slot_mask(tcnt_ref, g)
        points = tgt_ref[:, pl.ds(at, GS)]
        place, slots = order(points[1:2], live)
        tplace_ref[:, pl.ds(at, GS)] = place
        for h in range(CHUNKS):
            tlane_ref[:, pl.ds(at + h * LANES, LANES)] = gather(points, slots[h:h + 1])
        return 0

    lax.fori_loop(0, own, sort_target, 0)

    def windows(points_ref, at, count, g, acc, column):
        place = iota((8, LANES), 1) + iota((8, LANES), 0) * LANES
        y = jnp.concatenate(
            [points_ref[1:2, pl.ds(at + h * LANES, LANES)] for h in range(CHUNKS)], 0
        )
        low = jnp.min(jnp.where(place < count, y, jnp.inf), axis=1, keepdims=True) - R
        high = jnp.max(jnp.where(place < count, y, -jnp.inf), axis=1, keepdims=True) + R
        packed = jnp.zeros((8, 1), i32)
        steps = jnp.zeros((8, 1), i32)
        for b in range(3):
            there = g + b - 1
            yq = lane_ref[1:2, pl.ds(pl.multiple_of(there * GS, GS), GS)]
            n = live_total(scnt_ref, there)
            slot = jnp.broadcast_to(iota((1, GS), 1), (8, GS))
            near = (yq >= low) & (yq <= high) & (slot < n)
            slot = slot.astype(f32)
            first = jnp.min(jnp.where(near, slot, 4096.0), axis=1, keepdims=True).astype(i32)
            end = jnp.max(jnp.where(near, slot + 1.0, 0.0), axis=1, keepdims=True).astype(i32)
            unit = jnp.where(end > 0, first // 16, 0)
            packed = packed + unit * (128 ** b)
            steps = jnp.maximum(steps, (end - unit * 16 + WIN - 1) // WIN)
        packed = packed + steps * (128 ** 3)
        return jnp.where(iota((8, LANES), 1) == column, packed, acc)

    def source_windows(g, acc):
        return windows(lane_ref, pl.multiple_of(g * GS, GS), live_total(scnt_ref, g), g, acc, g)

    def target_windows(g, acc):
        return windows(
            tlane_ref, pl.multiple_of(g * GS, GS), live_total(tcnt_ref, g), g + HALO, acc, g + total
        )

    acc = lax.fori_loop(1, total - 1, source_windows, jnp.zeros((8, LANES), i32))
    wins_v[...] = lax.fori_loop(0, own, target_windows, acc)
    copy = pltpu.make_async_copy(wins_v, wins_s, sem)
    copy.start()
    copy.wait()

    def interact(points, packed, k, g, value_refs):
        acc = None
        for b in range(3):
            there = g + b - 1
            start = pl.multiple_of(jnp.minimum(((packed >> (7 * b)) & 127) * 16 + k * WIN, GS), 16)
            rows = rows_ref[pl.ds(pl.multiple_of(there * ROW_STRIDE + start, 16), WIN), :]
            square = None
            for axis in range(3):
                offset = rows[:, axis:axis + 1] - points[axis:axis + 1, :]
                square = offset * offset if axis == 0 else square + offset * offset
            square = jnp.minimum(jnp.maximum(square, 1e-30), float(R * R))
            distance = square * lax.rsqrt(square)
            rest = R - distance
            rest = rest * rest
            phi = rest * rest * (distance + 1.0)
            high, low = split(phi)
            parts = []
            for ref in value_refs:
                window = ref[:, pl.ds(pl.multiple_of(there * VAL_STRIDE + start // LANES * LANES, LANES), 384)]
                window = pltpu.roll(window, lax.rem(384 - start % LANES, 384), 1)[:, :WIN]
                parts += list(split(window))
            left = jnp.concatenate(parts, 0)
            term = dot(left, high) + dot(left, low)
            acc = term if acc is None else acc + term
        return acc

    def pass_over(column0, g0, groups, points_ref, cnt_ref, value_refs, store):
        rows_out = 2 * F * len(value_refs)

        def chunk(i, _):
            g = i // CHUNKS
            c = i % CHUNKS
            at = pl.multiple_of(i * LANES, LANES)
            packed = wins_s[c, g + column0]
            points = points_ref[:, pl.ds(at, LANES)]

            def step(k, acc):
                return acc + interact(points, packed, k, g + g0, value_refs)

            acc = lax.fori_loop(0, packed >> 21, step, jnp.zeros((rows_out, LANES), f32))
            here = (iota((F, LANES), 1) + c * LANES) < live_total(cnt_ref, g)
            for v in range(len(value_refs)):
                out = (acc[16 * v:16 * v + 8] + acc[16 * v + 8:16 * v + 16]) * (1.0 / 256.0)
                store(v, g, c, at, jnp.where(here, out, 0.0))
            return 0

        lax.fori_loop(groups[0] * CHUNKS, groups[1] * CHUNKS, chunk, 0)

    def store_w1(v, g, c, at, out):
        vw_ref[:, pl.ds(pl.multiple_of(g * VAL_STRIDE + c * LANES, LANES), LANES)] = out

    for g in (0, total - 1):
        vw_ref[:, g * VAL_STRIDE:g * VAL_STRIDE + GS] = jnp.zeros((F, GS), f32)
    pass_over(0, 0, (1, total - 1), lane_ref, scnt_ref, [vf_ref], store_w1)

    def store_w2(v, g, c, at, out):
        w2_ref[:, pl.ds(pl.multiple_of(at - HALO * GS, LANES), LANES)] = out

    pass_over(0, 0, (HALO, total - HALO), lane_ref, scnt_ref, [vw_ref], store_w2)

    def store_mapped(v, g, c, at, out):
        (mf_ref, mw_ref)[v][:, pl.ds(at, LANES)] = out

    pass_over(total, HALO, (0, own), tlane_ref, tcnt_ref, [vf_ref, vw_ref], store_mapped)

    def first_sums(g, acc):
        ff, fw = acc
        at = pl.multiple_of((g + HALO) * VAL_STRIDE, LANES)
        f = vf_ref[:, pl.ds(at, GS)]
        w = vw_ref[:, pl.ds(at, GS)]
        w1_ref[:, pl.ds(pl.multiple_of(g * GS, GS), GS)] = w
        return ff + f * f, fw + f * w

    zero = jnp.zeros((F, GS), f32)
    ff, fw = lax.fori_loop(0, own, first_sums, (zero, zero))
    ff = jnp.sum(ff, axis=1, keepdims=True)
    fw = jnp.sum(fw, axis=1, keepdims=True)
    shift = jnp.where(ff > 0, fw / jnp.where(ff > 0, ff, 1.0), 0.0)

    def second_sums(g, acc):
        ee, ez, fz = acc
        at = pl.multiple_of((g + HALO) * VAL_STRIDE, LANES)
        f = vf_ref[:, pl.ds(at, GS)]
        w = vw_ref[:, pl.ds(at, GS)]
        e = w - shift * f
        z = w2_ref[:, pl.ds(pl.multiple_of(g * GS, GS), GS)] - shift * w
        return ee + e * e, ez + e * z, fz + f * z

    sums = lax.fori_loop(0, own, second_sums, (zero, zero, zero))
    sums = [ff, shift] + [jnp.sum(s, axis=1, keepdims=True) for s in sums]
    mine = iota((F, LANES), 1) == me_ref[0]
    for n, value in enumerate(sums):
        sums_ref[n * F:(n + 1) * F, :] = jnp.where(mine, value, 0.0)


def final_kernel(
    scnt_ref, tcnt_ref, sums_ref, rhs_ref, splace_ref, tplace_ref, w1_ref, mf_ref, mw_ref, coef_ref, mapped_ref
):
    own = rhs_ref.shape[1] // GS
    ff, shift, ee, ez, fz = (sums_ref[n * F:(n + 1) * F, :] for n in range(5))

    def over(x):
        return jnp.sum(x, axis=1, keepdims=True)

    total = over(ff)
    mean = over(ff * shift) / total
    delta = shift - mean
    e_e = over(ee + delta * delta * ff)
    e_ae = over(ez + delta * (ee + fz) + delta * delta * shift * ff)
    alpha0 = 1.0 / mean
    ratio = e_e / total
    beta = alpha0 * alpha0 * ratio
    alpha1 = e_e / (e_ae - alpha0 * ratio * e_e)
    c1 = -alpha1 * alpha0
    c0 = alpha0 + alpha1 * (1.0 + beta)

    def group(g, _):
        at = pl.multiple_of(g * GS, GS)
        w = w1_ref[:, pl.ds(at, GS)]
        m = c0 * mf_ref[:, pl.ds(at, GS)] + c1 * mw_ref[:, pl.ds(at, GS)]
        f = rhs_ref[:, pl.ds(at, GS)]
        splace = splace_ref[:, pl.ds(pl.multiple_of(at + HALO * GS, GS), GS)]
        tplace = tplace_ref[:, pl.ds(at, GS)]
        slive = slot_mask(scnt_ref, g)
        tlive = slot_mask(tcnt_ref, g)
        for h in range(CHUNKS):
            lanes = slice(h * LANES, (h + 1) * LANES)
            coef = c0 * f[:, lanes] + c1 * gather(w, splace[:, lanes])
            coef_ref[:, pl.ds(at + h * LANES, LANES)] = jnp.where(slive[:, lanes], coef, 0.0)
            out = gather(m, tplace[:, lanes])
            mapped_ref[:, pl.ds(at + h * LANES, LANES)] = jnp.where(tlive[:, lanes], out, 0.0)
        return 0

    lax.fori_loop(0, own, group, 0)


def run_local(me, scnt, tcnt, src, tgt):
    points = tgt.shape[1]
    total = points // GS + 2 * HALO
    vmem = pl.BlockSpec(memory_space=pltpu.VMEM)
    smem = pl.BlockSpec(memory_space=pltpu.SMEM)
    return pl.pallas_call(
        local_kernel,
        out_shape=[
            jax.ShapeDtypeStruct((1, total * GS), i32),
            jax.ShapeDtypeStruct((1, points), i32),
            jax.ShapeDtypeStruct((F, points), f32),
            jax.ShapeDtypeStruct((F, points), f32),
            jax.ShapeDtypeStruct((F, points), f32),
            jax.ShapeDtypeStruct((5 * F, LANES), f32),
        ],
        in_specs=[smem, smem, smem, vmem, vmem],
        out_specs=[vmem] * 6,
        scratch_shapes=[
            pltpu.VMEM((total * ROW_STRIDE, LANES), f32),
            pltpu.VMEM((F, total * VAL_STRIDE), f32),
            pltpu.VMEM((F, total * VAL_STRIDE), f32),
            pltpu.VMEM((8, total * GS), f32),
            pltpu.VMEM((8, points), f32),
            pltpu.VMEM((F, points), f32),
            pltpu.VMEM((8, LANES), i32),
            pltpu.SMEM((8, LANES), i32),
            pltpu.SemaphoreType.DMA,
        ],
        compiler_params=pltpu.CompilerParams(vmem_limit_bytes=56 * 1024 * 1024),
        name="local",
    )(me, scnt, tcnt, src, tgt)


def run_final(scnt, tcnt, sums, rhs, splace, tplace, w1, mf, mw):
    vmem = pl.BlockSpec(memory_space=pltpu.VMEM)
    smem = pl.BlockSpec(memory_space=pltpu.SMEM)
    return pl.pallas_call(
        final_kernel,
        out_shape=[jax.ShapeDtypeStruct(rhs.shape, f32)] * 2,
        in_specs=[smem, smem] + [vmem] * 7,
        out_specs=[vmem] * 2,
        compiler_params=pltpu.CompilerParams(vmem_limit_bytes=40 * 1024 * 1024),
        name="final",
    )(scnt, tcnt, sums, rhs, splace, tplace, w1, mf, mw)


def shifted(x, by):
    peers = lax.axis_size(AXES)
    pairs = [(i, i + by) for i in range(peers) if 0 <= i + by < peers]
    return lax.ppermute(x, AXES, pairs)


def on_device(src_points, tgt_points, src_count, tgt_count, pair_list, pair_total, rhs):
    reach = HALO * GS
    blocks = HALO * R
    own = jnp.concatenate([rhs, src_points, jnp.zeros((5, rhs.shape[1]), f32)], 0)
    before = shifted(own[:11, -reach:], 1)
    after = shifted(own[:11, :reach], -1)
    pad = ((0, 5), (0, 0))
    src = jnp.concatenate([jnp.pad(before, pad), own, jnp.pad(after, pad)], 1)
    scnt = jnp.concatenate([shifted(src_count[-blocks:], 1), src_count, shifted(src_count[:blocks], -1)])
    tgt = jnp.pad(tgt_points, ((0, 5), (0, 0)))
    me = lax.axis_index(AXES).astype(i32)[None]
    splace, tplace, w1, mf, mw, sums = run_local(me, scnt, tgt_count, src, tgt)
    sums = lax.psum(sums, AXES)
    return run_final(src_count, tgt_count, sums, rhs, splace, tplace, w1, mf, mw)


def solution(mesh):
    return jax.shard_map(
        on_device,
        mesh=mesh,
        in_specs=(
            P(None, AXES),
            P(None, AXES),
            P(AXES),
            P(AXES),
            P(None, AXES),
            P(AXES),
            P(None, AXES),
        ),
        out_specs=(P(None, AXES), P(None, AXES)),
        check_vma=False,
    )
```

time: 2050 us -> 377 us (0.18)
  the two profiles are of different devices: /device:TPU:96 before, /device:TPU:1 now
where the time goes in v1:
time: 377 us; the launch traced here: 376 us
  Pallas kernels  260 us (69%)
  blocking collectives  89.5 us (24%)
  starting transfers between devices  12 us (3%)
  local copies, waits for them, and re-layouts  8.76 us (2%)
    pallas_call x1, Pallas kernels, run_local(): pl.pallas_call(local_kernel, out_shape=[jax.ShapeDtypeStruct((1, total *...  254 us
    psum x1, blocking collectives, on_device(): sums = lax.psum(sums, AXES)  89.5 us
    ppermute x4, starting transfers between devices, shifted(): return lax.ppermute(x, AXES, pairs)  12 us
  transfers between devices with their start and end apart: 4, of which 1 were waited for; matrix products, arithmetic and copies ran while one was open for 1% of the time, Pallas kernels for 0%

profile of v1, /device:TPU:1, one launch (start us, length us, event | category | flops | bytes accessed | tf_op | source)
XLA Modules:
  0.0 375.9 jit_solution(8294677036940602085)
XLA Ops:
  0.6 0.8 fusion.1
  1.4 4.5 %collective-permute-start = (s32[8]{0:T(128)S(1)}, s32[8]{0:T(128)S(1)}, u32[]{:S(2)}, u32[]{:S(2)}) collective-permute-start(s32[8]{0:T(128)S(1)} %get-tuple-element.16), channel_id=1, source_target_pairs={{0,1},{1,2},{2,3},{3,4},{4,5},{5,6},{6,7},{7,8},{8,9},{9,10},{10,1... | collective-permute-start | bytes 104 | tf_op jit(solution)/shard_map/ppermute | solution.py:376
  5.9 0.0 copy-start.6
  6.0 1.9 collective-permute-start.1
  7.9 1.1 constant_dynamic-update-slice_fusion.1
  9.0 0.0 copy-start
  9.0 0.0 copy-start.8
  9.0 1.1 constant_dynamic-update-slice_fusion
  10.1 3.6 collective-permute-start.2
  13.8 1.9 collective-permute-start.3
  15.7 0.8 pad.13.tgt_ref
  16.6 0.0 collective-permute-done
  16.6 0.0 collective-permute-done.1
  16.6 0.6 pad_add_fusion.scnt_ref
  17.2 2.9 collective-permute-done.3
  20.1 1.2 select_maximum_fusion.src_ref
  21.4 254.1 %local.1 = (s32[1,20480]{1,0:T(1,128)}, s32[1,16384]{1,0:T(1,128)}, f32[8,16384]{1,0:T(8,128)}, f32[8,16384]{1,0:T(8,128)}, f32[8,16384]{1,0:T(8,128)}, /*index=5*/f32[40,128]{1,0:T(8,128)}) custom-call(s32[1]{0:T(128)} %bitcast.me_ref, s32[80]{0:T(128)} %pad_add_fusion.scnt_ref, s32[64]{0:T(128)} %tcnt_ref.3, f32[16,20480]{1,0:T(8,128)} %select_maximum_fusion.src_ref, ...), custom_call_target="tpu_custom_call" | custom-call | tf_op jit(solution)/shard_map/local/pallas_call | solution.py:332
  275.5 89.5 %psum.7.sums_ref = f32[40,128]{1,0:T(8,128)S(1)} all-reduce(f32[40,128]{1,0:T(8,128)} %get-tuple-element.8), channel_id=1, replica_groups=mesh['src'=16,'tgt'=8] {'src','tgt'}, use_global_device_ids=true, to_apply=%region_0.1 | all-reduce | flops 5120 | bytes 40960 | tf_op jit(solution)/shard_map/psum | solution.py:391
  365.0 1.0 copy-done.1
  366.0 1.0 copy-done.2
  367.1 1.0 copy-done.3
  368.1 0.9 copy-done.4
  369.0 0.8 copy-done.5
  369.9 6.0 %final.1 = (f32[8,16384]{1,0:T(8,128)}, f32[8,16384]{1,0:T(8,128)}) custom-call(s32[64]{0:T(128)S(1)} %copy-done.6, s32[64]{0:T(128)S(1)} %copy-done.7, f32[40,128]{1,0:T(8,128)S(1)} %psum.7.sums_ref, f32[8,16384]{1,0:T(8,128)S(1)} %copy-done, s32[1,20480]{1,0:T(1,128)S(1)} %copy-done.4, s32[1,16384]{1,0:T(1,128)S(1)} %copy-done.5, ...), custom_call_target="tpu_custom_call" | custom-call | tf_op jit(solution)/shard_map/final/pallas_call | solution.py:363
  (15 shorter events, 0.1 us)
Async XLA Ops:
  0.6 15.1 %copy-start.9 = (f32[3,16384]{1,0:T(4,128)S(1)}, f32[3,16384]{1,0:T(4,128)}, u32[]{:S(2)}) copy-start(f32[3,16384]{1,0:T(4,128)} %param.8) | copy-start | bytes 589828
  1.4 15.1 %collective-permute-start = (s32[8]{0:T(128)S(1)}, s32[8]{0:T(128)S(1)}, u32[]{:S(2)}, u32[]{:S(2)}) collective-permute-start(s32[8]{0:T(128)S(1)} %get-tuple-element.16), channel_id=1, source_target_pairs={{0,1},{1,2},{2,3},{3,4},{4,5},{5,6},{6,7},{7,8},{8,9},{9,10},{10,1... | collective-permute-start | bytes 104 | tf_op jit(solution)/shard_map/ppermute | solution.py:376
  5.9 10.6 %copy-start.6 = (s32[64]{0:T(128)S(1)}, s32[64]{0:T(128)}, u32[]{:S(2)}) copy-start(s32[64]{0:T(128)} %scnt_ref.1) | copy-start | bytes 772
  6.0 10.6 %collective-permute-start.1 = (s32[8]{0:T(128)S(1)}, s32[8]{0:T(128)S(1)}, u32[]{:S(2)}, u32[]{:S(2)}) collective-permute-start(s32[8]{0:T(128)S(1)} %get-tuple-element.17), channel_id=1, source_target_pairs={{1,0},{2,1},{3,2},{4,3},{5,4},{6,5},{7,6},{8,7},{9,8},{10,9},{11,1... | collective-permute-start | bytes 104 | tf_op jit(solution)/shard_map/ppermute | solution.py:376
  9.0 11.1 %copy-start = (f32[8,16384]{1,0:T(8,128)S(1)}, f32[8,16384]{1,0:T(8,128)}, u32[]{:S(2)}) copy-start(f32[8,16384]{1,0:T(8,128)} %rhs_ref.1) | copy-start | bytes 1572868
  9.0 11.1 %copy-start.8 = (f32[3,16384]{1,0:T(4,128)S(1)}, f32[3,16384]{1,0:T(4,128)}, u32[]{:S(2)}) copy-start(f32[3,16384]{1,0:T(4,128)} %param.7) | copy-start | bytes 589828
  10.1 7.0 %collective-permute-start.2 = (f32[11,2048]{1,0:T(8,128)S(1)}, f32[11,2048]{1,0:T(8,128)S(1)}, u32[]{:S(2)}, u32[]{:S(2)}) collective-permute-start(f32[11,2048]{1,0:T(8,128)S(1)} %get-tuple-element.14), channel_id=1, source_target_pairs={{0,1},{1,2},{2,3},{3,4},{4,5},{5,6},{6,7},{7,8},{8,9},{9,10},{10,1... | collective-permute-start | bytes 270344 | tf_op jit(solution)/shard_map/ppermute | solution.py:376
  13.8 6.3 %collective-permute-start.3 = (f32[11,2048]{1,0:T(8,128)S(1)}, f32[11,2048]{1,0:T(8,128)S(1)}, u32[]{:S(2)}, u32[]{:S(2)}) collective-permute-start(f32[11,2048]{1,0:T(8,128)S(1)} %get-tuple-element.15), channel_id=1, source_target_pairs={{1,0},{2,1},{3,2},{4,3},{5,4},{6,5},{7,6},{8,7},{9,8},{10,9},{11,1... | collective-permute-start | bytes 270344 | tf_op jit(solution)/shard_map/ppermute | solution.py:376
  21.4 343.6 %copy-start.7 = (s32[64]{0:T(128)S(1)}, s32[64]{0:T(128)}, u32[]{:S(2)}) copy-start(s32[64]{0:T(128)} %tcnt_ref.3) | copy-start | bytes 772
  365.0 1.0 copy-start.1
  366.0 1.0 copy-start.2
  367.1 1.0 copy-start.3
  368.1 0.9 copy-start.4
  369.0 0.8 copy-start.5

commit v2 on v1

--- a/solution.py
+++ b/solution.py
@@ -19,6 +19,7 @@
 ROW_STRIDE = GS + WIN
 VAL_STRIDE = GS + 384
 SEG = 256
+BATCH = 4
 AXES = ("src", "tgt")
 f32 = jnp.float32
 bf16 = jnp.bfloat16
@@ -101,26 +102,37 @@
 
 
 def local_kernel(
-    me_ref, scnt_ref, tcnt_ref, src_ref, tgt_ref,
+    scnt_ref, tcnt_ref, before_ref, after_ref, rhs_ref, points_ref, tgt_ref,
     splace_ref, tplace_ref, w1_ref, mf_ref, mw_ref, sums_ref,
-    rows_ref, vf_ref, vw_ref, lane_ref, tlane_ref, w2_ref, wins_v, wins_s, sem,
+    src_ref, rows_ref, vf_ref, vw_ref, lane_ref, tlane_ref, w2_ref, wins_v, wins_s, list_s, sem,
 ):
     own = tgt_ref.shape[1] // GS
     total = own + 2 * HALO
 
+    reach = HALO * GS
+    points = tgt_ref.shape[1]
+    for at, refs in ((0, (before_ref,)), (reach, (rhs_ref, points_ref)), (reach + points, (after_ref,))):
+        row = 0
+        for ref in refs:
+            src_ref[row:row + min(ref.shape[0], 11), at:at + ref.shape[1]] = ref[:11, :]
+            row += ref.shape[0]
+
     def clear(g, _):
-        rows_ref[pl.ds(pl.multiple_of(g * ROW_STRIDE + GS, 8), WIN), :] = jnp.zeros((WIN, LANES), f32)
+        rows_ref[:, pl.ds(pl.multiple_of(g * ROW_STRIDE + GS, 8), WIN), :] = jnp.zeros((3, WIN, LANES), f32)
         vf_ref[:, pl.ds(pl.multiple_of(g * VAL_STRIDE + GS, LANES), 384)] = jnp.zeros((F, 384), f32)
-        vw_ref[:, pl.ds(pl.multiple_of(g * VAL_STRIDE + GS, LANES), 384)] = jnp.zeros((F, 384), f32)
+        vw_ref[:, pl.ds(pl.multiple_of(g * VAL_STRIDE, LANES), VAL_STRIDE)] = jnp.zeros((F, VAL_STRIDE), f32)
         return 0
 
     lax.fori_loop(0, total, clear, 0)
+    w2_ref[...] = jnp.zeros_like(w2_ref)
+    mf_ref[...] = jnp.zeros_like(mf_ref)
+    mw_ref[...] = jnp.zeros_like(mw_ref)
 
     def sort_source(g, _):
         at = pl.multiple_of(g * GS, GS)
         live = slot_mask(scnt_ref, g)
         count = live_total(scnt_ref, g)
-        points = src_ref[8:16, pl.ds(at, GS)]
+        points = jnp.concatenate([src_ref[8:11, pl.ds(at, GS)], jnp.zeros((5, GS), f32)], 0)
         field = src_ref[0:8, pl.ds(at, GS)]
         place, slots = order(points[1:2], live)
         splace_ref[:, pl.ds(at, GS)] = place
@@ -130,7 +142,10 @@
             moved = gather(points, index)
             lane_ref[:, pl.ds(at + h * LANES, LANES)] = moved
             wide = jnp.concatenate([moved, jnp.zeros((LANES - 8, LANES), f32)], 0)
-            rows_ref[pl.ds(pl.multiple_of(g * ROW_STRIDE + h * LANES, 8), LANES), :] = wide.T
+            wide = wide.T
+            row = pl.multiple_of(g * ROW_STRIDE + h * LANES, 8)
+            for axis in range(3):
+                rows_ref[axis, pl.ds(row, LANES), :] = jnp.broadcast_to(wide[:, axis:axis + 1], (LANES, LANES))
             vf_ref[:, pl.ds(pl.multiple_of(g * VAL_STRIDE + h * LANES, LANES), LANES)] = jnp.where(
                 here, gather(field, index), 0.0
             )
@@ -141,7 +156,7 @@
     def sort_target(g, _):
         at = pl.multiple_of(g * GS, GS)
         live = slot_mask(tcnt_ref, g)
-        points = tgt_ref[:, pl.ds(at, GS)]
+        points = jnp.concatenate([tgt_ref[:, pl.ds(at, GS)], jnp.zeros((5, GS), f32)], 0)
         place, slots = order(points[1:2], live)
         tplace_ref[:, pl.ds(at, GS)] = place
         for h in range(CHUNKS):
@@ -193,10 +208,10 @@
         for b in range(3):
             there = g + b - 1
             start = pl.multiple_of(jnp.minimum(((packed >> (7 * b)) & 127) * 16 + k * WIN, GS), 16)
-            rows = rows_ref[pl.ds(pl.multiple_of(there * ROW_STRIDE + start, 16), WIN), :]
+            row = pl.multiple_of(there * ROW_STRIDE + start, 16)
             square = None
             for axis in range(3):
-                offset = rows[:, axis:axis + 1] - points[axis:axis + 1, :]
+                offset = rows_ref[axis, pl.ds(row, WIN), :] - points[axis:axis + 1, :]
                 square = offset * offset if axis == 0 else square + offset * offset
             square = jnp.minimum(jnp.maximum(square, 1e-30), float(R * R))
             distance = square * lax.rsqrt(square)
@@ -210,37 +225,53 @@
                 window = pltpu.roll(window, lax.rem(384 - start % LANES, 384), 1)[:, :WIN]
                 parts += list(split(window))
             left = jnp.concatenate(parts, 0)
-            term = dot(left, high) + dot(left, low)
+            term = dot(left, jnp.concatenate([high, low], 1))
             acc = term if acc is None else acc + term
-        return acc
+        return acc[:, :LANES] + acc[:, LANES:]
 
     def pass_over(column0, g0, groups, points_ref, cnt_ref, value_refs, store):
         rows_out = 2 * F * len(value_refs)
 
-        def chunk(i, _):
-            g = i // CHUNKS
-            c = i % CHUNKS
-            at = pl.multiple_of(i * LANES, LANES)
-            packed = wins_s[c, g + column0]
-            points = points_ref[:, pl.ds(at, LANES)]
-
-            def step(k, acc):
-                return acc + interact(points, packed, k, g + g0, value_refs)
-
-            acc = lax.fori_loop(0, packed >> 21, step, jnp.zeros((rows_out, LANES), f32))
-            here = (iota((F, LANES), 1) + c * LANES) < live_total(cnt_ref, g)
-            for v in range(len(value_refs)):
-                out = (acc[16 * v:16 * v + 8] + acc[16 * v + 8:16 * v + 16]) * (1.0 / 256.0)
-                store(v, g, c, at, jnp.where(here, out, 0.0))
+        def list_group(g, n):
+            def list_chunk(c, n):
+                list_s[n] = g * CHUNKS + c
+                return n + 1
+
+            return lax.fori_loop(0, (live_total(cnt_ref, g) + LANES - 1) // LANES, list_chunk, n)
+
+        n = lax.fori_loop(groups[0], groups[1], list_group, 0)
+
+        def batch(i, _):
+            work = []
+            for u in range(BATCH):
+                item = list_s[jnp.minimum(i * BATCH + u, n - 1)]
+                g = item // CHUNKS
+                c = item % CHUNKS
+                at = pl.multiple_of(item * LANES, LANES)
+                packed = wins_s[c, g + column0]
+                work.append((g, c, at, packed, points_ref[:, pl.ds(at, LANES)]))
+            accs = tuple(interact(points, packed, 0, g + g0, value_refs) for g, c, at, packed, points in work)
+            most = functools.reduce(jnp.maximum, [w[3] >> 21 for w in work])
+
+            def step(k, accs):
+                return tuple(
+                    acc + interact(points, packed, k, g + g0, value_refs)
+                    for acc, (g, c, at, packed, points) in zip(accs, work)
+                )
+
+            accs = lax.fori_loop(1, most, step, accs)
+            for acc, (g, c, at, packed, points) in zip(accs, work):
+                here = (iota((F, LANES), 1) + c * LANES) < live_total(cnt_ref, g)
+                for v in range(len(value_refs)):
+                    out = (acc[16 * v:16 * v + 8] + acc[16 * v + 8:16 * v + 16]) * (1.0 / 256.0)
+                    store(v, g, c, at, jnp.where(here, out, 0.0))
             return 0
 
-        lax.fori_loop(groups[0] * CHUNKS, groups[1] * CHUNKS, chunk, 0)
+        lax.fori_loop(0, (n + BATCH - 1) // BATCH, batch, 0)
 
     def store_w1(v, g, c, at, out):
         vw_ref[:, pl.ds(pl.multiple_of(g * VAL_STRIDE + c * LANES, LANES), LANES)] = out
 
-    for g in (0, total - 1):
-        vw_ref[:, g * VAL_STRIDE:g * VAL_STRIDE + GS] = jnp.zeros((F, GS), f32)
     pass_over(0, 0, (1, total - 1), lane_ref, scnt_ref, [vf_ref], store_w1)
 
     def store_w2(v, g, c, at, out):
@@ -278,31 +309,96 @@
 
     sums = lax.fori_loop(0, own, second_sums, (zero, zero, zero))
     sums = [ff, shift] + [jnp.sum(s, axis=1, keepdims=True) for s in sums]
-    mine = iota((F, LANES), 1) == me_ref[0]
+    tile = jnp.zeros((F, LANES), f32)
     for n, value in enumerate(sums):
-        sums_ref[n * F:(n + 1) * F, :] = jnp.where(mine, value, 0.0)
-
-
-def final_kernel(
-    scnt_ref, tcnt_ref, sums_ref, rhs_ref, splace_ref, tplace_ref, w1_ref, mf_ref, mw_ref, coef_ref, mapped_ref
-):
-    own = rhs_ref.shape[1] // GS
-    ff, shift, ee, ez, fz = (sums_ref[n * F:(n + 1) * F, :] for n in range(5))
+        tile = jnp.where(iota((F, LANES), 1) == n, value, tile)
+    sums_ref[...] = jnp.concatenate([tile, jnp.zeros((LANES - F, LANES), f32)], 0).T[:8]
+
+
+def merge(tiles):
+    ff, shift, ee, ez, fz = (tiles[:, n, :] for n in range(5))
 
     def over(x):
-        return jnp.sum(x, axis=1, keepdims=True)
+        return jnp.sum(x, axis=0, keepdims=True)
 
     total = over(ff)
-    mean = over(ff * shift) / total
+    mean = over(ff * shift) / jnp.where(total > 0, total, 1.0)
     delta = shift - mean
-    e_e = over(ee + delta * delta * ff)
-    e_ae = over(ez + delta * (ee + fz) + delta * delta * shift * ff)
+    fw = shift * ff
+    return [
+        total,
+        mean,
+        over(ee + delta * delta * ff),
+        over(ez + delta * (ee + fz) + delta * delta * fw),
+        over(fz + delta * fw),
+    ]
+
+
+def share_kernel(sums_ref, out_ref, first, second, send1, recv1, send2, recv2):
+    me = [lax.axis_index(name) for name in AXES]
+    sizes = (second.shape[0], first.shape[0])
+
+    def peer(axis, by):
+        return {AXES[axis]: lax.rem(me[axis] + by, sizes[axis])}
+
+    barrier = pltpu.get_barrier_semaphore()
+    for axis in (0, 1):
+        for by in range(1, sizes[axis]):
+            pl.semaphore_signal(
+                barrier, inc=1, device_id=peer(axis, by), device_id_type=pl.DeviceIdType.MESH
+            )
+    pl.semaphore_wait(barrier, sizes[0] + sizes[1] - 2)
+
+    def exchange(axis, slots, send, recv):
+        copies = []
+        for by in range(1, sizes[axis]):
+            copy = pltpu.make_async_remote_copy(
+                src_ref=slots.at[0],
+                dst_ref=slots.at[by],
+                send_sem=send.at[by],
+                recv_sem=recv.at[by],
+                device_id=peer(axis, by),
+                device_id_type=pl.DeviceIdType.MESH,
+            )
+            copy.start()
+            copies.append(copy)
+        for copy in copies:
+            copy.wait()
+
+    first[0] = sums_ref[...]
+    exchange(1, first, send1, recv1)
+    part = merge(first[...])
+    second[0] = jnp.concatenate(part + [jnp.zeros((3, LANES), f32)], 0)
+    exchange(0, second, send2, recv2)
+    total, mean, e_e, e_ae, _ = merge(second[...])
     alpha0 = 1.0 / mean
     ratio = e_e / total
     beta = alpha0 * alpha0 * ratio
     alpha1 = e_e / (e_ae - alpha0 * ratio * e_e)
     c1 = -alpha1 * alpha0
     c0 = alpha0 + alpha1 * (1.0 + beta)
+    out_ref[...] = jnp.concatenate([c0, c1, jnp.zeros((LANES - 2, LANES), f32)], 0).T[:F]
+
+
+def final_kernel(
+    scnt_ref, tcnt_ref, scale_ref, rhs_hbm, splace_hbm, tplace_hbm, w1_hbm, mf_hbm, mw_hbm,
+    coef_ref, mapped_ref,
+    rhs_ref, splace_ref, tplace_ref, w1_ref, mf_ref, mw_ref, sems,
+):
+    copies = [
+        pltpu.make_async_copy(here, there, sems.at[n])
+        for n, (here, there) in enumerate([
+            (rhs_hbm, rhs_ref), (splace_hbm, splace_ref), (tplace_hbm, tplace_ref),
+            (w1_hbm, w1_ref), (mf_hbm, mf_ref), (mw_hbm, mw_ref),
+        ])
+    ]
+    for copy in copies:
+        copy.start()
+    for copy in copies:
+        copy.wait()
+    own = rhs_ref.shape[1] // GS
+    c0 = scale_ref[:, 0:1]
+    c1 = scale_ref[:, 1:2]
 
     def group(g, _):
         at = pl.multiple_of(g * GS, GS)
@@ -324,7 +420,7 @@
     lax.fori_loop(0, own, group, 0)
 
 
-def run_local(me, scnt, tcnt, src, tgt):
+def run_local(scnt, tcnt, before, after, rhs, src, tgt):
     points = tgt.shape[1]
     total = points // GS + 2 * HALO
     vmem = pl.BlockSpec(memory_space=pltpu.VMEM)
@@ -337,12 +433,13 @@
             jax.ShapeDtypeStruct((F, points), f32),
             jax.ShapeDtypeStruct((F, points), f32),
             jax.ShapeDtypeStruct((F, points), f32),
-            jax.ShapeDtypeStruct((5 * F, LANES), f32),
+            jax.ShapeDtypeStruct((8, LANES), f32),
         ],
-        in_specs=[smem, smem, smem, vmem, vmem],
+        in_specs=[smem, smem] + [vmem] * 5,
         out_specs=[vmem] * 6,
         scratch_shapes=[
-            pltpu.VMEM((total * ROW_STRIDE, LANES), f32),
+            pltpu.VMEM((16, total * GS), f32),
+            pltpu.VMEM((3, total * ROW_STRIDE, LANES), f32),
             pltpu.VMEM((F, total * VAL_STRIDE), f32),
             pltpu.VMEM((F, total * VAL_STRIDE), f32),
             pltpu.VMEM((8, total * GS), f32),
@@ -350,24 +447,48 @@
             pltpu.VMEM((F, points), f32),
             pltpu.VMEM((8, LANES), i32),
             pltpu.SMEM((8, LANES), i32),
+            pltpu.SMEM((total * CHUNKS,), i32),
             pltpu.SemaphoreType.DMA,
         ],
         compiler_params=pltpu.CompilerParams(vmem_limit_bytes=56 * 1024 * 1024),
         name="local",
-    )(me, scnt, tcnt, src, tgt)
-
-
-def run_final(scnt, tcnt, sums, rhs, splace, tplace, w1, mf, mw):
+    )(scnt, tcnt, before, after, rhs, src, tgt)
+
+
+def run_share(sums, sizes):
+    vmem = pl.BlockSpec(memory_space=pltpu.VMEM)
+    return pl.pallas_call(
+        share_kernel,
+        out_shape=jax.ShapeDtypeStruct((F, LANES), f32),
+        in_specs=[vmem],
+        out_specs=vmem,
+        scratch_shapes=[
+            pltpu.VMEM((sizes[1], 8, LANES), f32),
+            pltpu.VMEM((sizes[0], 8, LANES), f32),
+            pltpu.SemaphoreType.DMA((sizes[1],)),
+            pltpu.SemaphoreType.DMA((sizes[1],)),
+            pltpu.SemaphoreType.DMA((sizes[0],)),
+            pltpu.SemaphoreType.DMA((sizes[0],)),
+        ],
+        compiler_params=pltpu.CompilerParams(collective_id=1, has_side_effects=True),
+        name="share",
+    )(sums)
+
+
+def run_final(scnt, tcnt, scale, *arrays):
     vmem = pl.BlockSpec(memory_space=pltpu.VMEM)
     smem = pl.BlockSpec(memory_space=pltpu.SMEM)
+    anywhere = pl.BlockSpec(memory_space=pl.ANY)
     return pl.pallas_call(
         final_kernel,
-        out_shape=[jax.ShapeDtypeStruct(rhs.shape, f32)] * 2,
-        in_specs=[smem, smem] + [vmem] * 7,
+        out_shape=[jax.ShapeDtypeStruct(arrays[0].shape, f32)] * 2,
+        in_specs=[smem, smem, vmem] + [anywhere] * len(arrays),
         out_specs=[vmem] * 2,
-        compiler_params=pltpu.CompilerParams(vmem_limit_bytes=40 * 1024 * 1024),
+        scratch_shapes=[pltpu.VMEM(a.shape, a.dtype) for a in arrays]
+        + [pltpu.SemaphoreType.DMA((len(arrays),))],
+        compiler_params=pltpu.CompilerParams(vmem_limit_bytes=60 * 1024 * 1024),
         name="final",
-    )(scnt, tcnt, sums, rhs, splace, tplace, w1, mf, mw)
+    )(scnt, tcnt, scale, *arrays)
 
 
 def shifted(x, by):
@@ -379,17 +500,17 @@
 def on_device(src_points, tgt_points, src_count, tgt_count, pair_list, pair_total, rhs):
     reach = HALO * GS
     blocks = HALO * R
-    own = jnp.concatenate([rhs, src_points, jnp.zeros((5, rhs.shape[1]), f32)], 0)
-    before = shifted(own[:11, -reach:], 1)
-    after = shifted(own[:11, :reach], -1)
-    pad = ((0, 5), (0, 0))
-    src = jnp.concatenate([jnp.pad(before, pad), own, jnp.pad(after, pad)], 1)
-    scnt = jnp.concatenate([shifted(src_count[-blocks:], 1), src_count, shifted(src_count[:blocks], -1)])
-    tgt = jnp.pad(tgt_points, ((0, 5), (0, 0)))
-    me = lax.axis_index(AXES).astype(i32)[None]
-    splace, tplace, w1, mf, mw, sums = run_local(me, scnt, tgt_count, src, tgt)
-    sums = lax.psum(sums, AXES)
-    return run_final(src_count, tgt_count, sums, rhs, splace, tplace, w1, mf, mw)
+    counts = src_count.astype(f32)
+    edges = [
+        jnp.concatenate([rhs[:, part], src_points[:, part], jnp.pad(counts[rows], (0, reach - blocks))[None]], 0)
+        for part, rows in ((slice(-reach, None), slice(-blocks, None)), (slice(0, reach), slice(0, blocks)))
+    ]
+    before = shifted(edges[0], 1)
+    after = shifted(edges[1], -1)
+    scnt = jnp.concatenate([before[11, :blocks].astype(i32), src_count, after[11, :blocks].astype(i32)])
+    splace, tplace, w1, mf, mw, sums = run_local(scnt, tgt_count, before, after, rhs, src_points, tgt_points)
+    scale = run_share(sums, [lax.axis_size(name) for name in AXES])
+    return run_final(src_count, tgt_count, scale, rhs, splace, tplace, w1, mf, mw)
 
 
 def solution(mesh):

time: 377 us -> 244 us (0.65)
  blocking collectives: 89.5 us -> 0 us
  Pallas kernels: 260 us -> 232 us
  local copies, waits for them, and re-layouts: 8.76 us -> 1.77 us
  starting transfers between devices: 12 us -> 6.43 us
    psum x1 -> x0, blocking collectives: 89.5 us -> none  [on_device(): sums = lax.psum(sums, AXES)]
    pallas_call x1, Pallas kernels: 254 us -> 198 us  [run_local(): pl.pallas_call(local_kernel, out_shape=[jax.ShapeDtypeStruct((1, total *...]
    pallas_call x1 -> x2, Pallas kernels: 6.04 us -> 33.8 us  [the longest x1 25.9 us: run_share(): pl.pallas_call(share_kernel, out_shape=jax.ShapeDtypeStruct((F, LANES), f...]
    unnamed x21 -> x6, local copies, waits for them, and re-layouts: 5.95 us -> 0.01 us
    ppermute x4 -> x2, starting transfers between devices: 12 us -> 6.43 us  [shifted(): return lax.ppermute(x, AXES, pairs)]
  transfers between devices with their start and end apart: 4 -> 2, of which waited for: 1 -> 2; matrix products, arithmetic and copies ran while one was open for 1% -> 0% of each run, Pallas kernels for 0% -> 0%
where the time goes in v2:
time: 244 us
  Pallas kernels  232 us (95%)
  starting transfers between devices  6.43 us (3%)
    pallas_call x1, Pallas kernels, run_local(): pl.pallas_call(local_kernel, out_shape=[jax.ShapeDtypeStruct((1, total *...  198 us
    pallas_call x1, Pallas kernels, run_share(): pl.pallas_call(share_kernel, out_shape=jax.ShapeDtypeStruct((F, LANES), f...  25.9 us
    pallas_call x1, Pallas kernels, run_final(): pl.pallas_call(final_kernel, out_shape=[jax.ShapeDtypeStruct(arrays[0].sh...  7.85 us
    ppermute x2, starting transfers between devices, shifted(): return lax.ppermute(x, AXES, pairs)  6.43 us
  transfers between devices with their start and end apart: 2, of which 2 were waited for; matrix products, arithmetic and copies ran while one was open for 0% of the time, Pallas kernels for 0%

profile of v2, /device:TPU:1, one launch (start us, length us, event | category | flops | bytes accessed | tf_op | source)
XLA Modules:
  0.0 243.9 jit_solution(2648597923592304085)
XLA Ops:
  0.6 0.7 convert_element_type.18
  1.3 0.1 fusion.4
  1.4 0.8 fusion.3
  2.2 0.9 fusion.2
  3.1 3.3 %collective-permute-start.1 = (f32[12,2048]{1,0:T(8,128)S(1)}, f32[12,2048]{1,0:T(8,128)S(1)}, u32[]{:S(2)}, u32[]{:S(2)}) collective-permute-start(f32[12,2048]{1,0:T(8,128)S(1)} %pad_maximum_fusion.1), channel_id=1, source_target_pairs={{1,0},{2,1},{3,2},{4,3},{5,4},{6,5},{7,6},{8,7},{9,8},{10,9},{11,1... | collective-permute-start | bytes 294920 | tf_op jit(solution)/shard_map/ppermute | solution.py:497
  6.5 3.1 %collective-permute-start = (f32[12,2048]{1,0:T(8,128)S(1)}, f32[12,2048]{1,0:T(8,128)S(1)}, u32[]{:S(2)}, u32[]{:S(2)}) collective-permute-start(f32[12,2048]{1,0:T(8,128)S(1)} %pad_maximum_fusion), channel_id=1, source_target_pairs={{0,1},{1,2},{2,3},{3,4},{4,5},{5,6},{6,7},{7,8},{8,9},{9,10},{10,1... | collective-permute-start | bytes 294920 | tf_op jit(solution)/shard_map/ppermute | solution.py:497
  9.6 0.7 collective-permute-done.1.after_ref
  10.2 0.0 copy-start
  10.2 0.0 copy-start.2
  10.3 1.2 collective-permute-done.before_ref
  11.5 0.0 copy-start.1
  11.5 0.0 copy-done.2
  11.5 0.6 pad_add_fusion.scnt_ref
  12.1 0.0 copy-done
  12.2 0.0 copy-done.1
  12.2 198.0 %local.1 = (s32[1,20480]{1,0:T(1,128)}, s32[1,16384]{1,0:T(1,128)}, f32[8,16384]{1,0:T(8,128)}, f32[8,16384]{1,0:T(8,128)}, f32[8,16384]{1,0:T(8,128)}, /*index=5*/f32[8,128]{1,0:T(8,128)}) custom-call(s32[80]{0:T(128)} %pad_add_fusion.scnt_ref, s32[64]{0:T(128)} %tcnt_ref.3, f32[12,2048]{1,0:T(8,128)} %copy-done.1, f32[12,2048]{1,0:T(8,128)} %copy-done, ...), custom_call_target="tpu_custom_call" | custom-call | tf_op jit(solution)/shard_map/local/pallas_call | solution.py:428
  210.2 25.9 %share.1.scale_ref = f32[8,128]{1,0:T(8,128)} custom-call(f32[8,128]{1,0:T(8,128)} %get-tuple-element.8.sums_ref), custom_call_target="tpu_custom_call" | custom-call | tf_op jit(solution)/shard_map/share/pallas_call | solution.py:460
  236.1 7.8 %final.1 = (f32[8,16384]{1,0:T(8,128)}, f32[8,16384]{1,0:T(8,128)}) custom-call(s32[64]{0:T(128)} %scnt_ref.1, s32[64]{0:T(128)} %tcnt_ref.3, f32[8,128]{1,0:T(8,128)} %share.1.scale_ref, f32[8,16384]{1,0:T(8,128)} %rhs_hbm.1, s32[1,20480]{1,0:T(1,128)} %get-tuple-element.9.splace_hbm, s32[1,16384]{1,0:T(1,128)} %get-tuple-element.10.tplace_hbm, ...), custom_call_target="tpu_custom_call" | custom-call | tf_op jit(solution)/shard_map/final/pallas_call | solution.py:482
  (6 shorter events, 0.1 us)
Async XLA Ops:
  3.1 7.2 %collective-permute-start.1 = (f32[12,2048]{1,0:T(8,128)S(1)}, f32[12,2048]{1,0:T(8,128)S(1)}, u32[]{:S(2)}, u32[]{:S(2)}) collective-permute-start(f32[12,2048]{1,0:T(8,128)S(1)} %pad_maximum_fusion.1), channel_id=1, source_target_pairs={{1,0},{2,1},{3,2},{4,3},{5,4},{6,5},{7,6},{8,7},{9,8},{10,9},{11,1... | collective-permute-start | bytes 294920 | tf_op jit(solution)/shard_map/ppermute | solution.py:497
  6.5 5.0 %collective-permute-start = (f32[12,2048]{1,0:T(8,128)S(1)}, f32[12,2048]{1,0:T(8,128)S(1)}, u32[]{:S(2)}, u32[]{:S(2)}) collective-permute-start(f32[12,2048]{1,0:T(8,128)S(1)} %pad_maximum_fusion), channel_id=1, source_target_pairs={{0,1},{1,2},{2,3},{3,4},{4,5},{5,6},{6,7},{7,8},{8,9},{9,10},{10,1... | collective-permute-start | bytes 294920 | tf_op jit(solution)/shard_map/ppermute | solution.py:497
  10.2 1.9 copy-start
  10.2 1.3 copy-start.2
  11.5 0.7 copy-start.1

commit v3 on v2

--- a/solution.py
+++ b/solution.py
@@ -1,5 +1,3 @@
-import functools
-
 import jax
 import jax.numpy as jnp
 from jax import lax
@@ -16,10 +14,13 @@
 CHUNKS = GS // LANES
 BINS = 128
 WIN = 192
+MORE = 64
 ROW_STRIDE = GS + WIN
 VAL_STRIDE = GS + 384
 SEG = 256
 BATCH = 4
+LAG = -(-15 // BATCH) + 1
+TOGETHER = 4
 AXES = ("src", "tgt")
 f32 = jnp.float32
 bf16 = jnp.bfloat16
@@ -50,39 +51,52 @@
     return total
 
 
-def order(y, live):
-    low = jnp.min(jnp.where(live, y, jnp.inf))
-    high = jnp.max(jnp.where(live, y, -jnp.inf))
+def order(y, live, upper, lower):
+    low = jnp.min(jnp.where(live, y, jnp.inf), axis=1, keepdims=True)
+    high = jnp.max(jnp.where(live, y, -jnp.inf), axis=1, keepdims=True)
     scale = BINS / jnp.maximum(high - low, 1e-30)
     scaled = jnp.minimum(jnp.maximum((y - low) * scale, 0.0), BINS - 1.0)
     bin_of = jnp.where(live, scaled.astype(i32), BINS)
-    ones_col = iota((SEG, SEG + LANES), 1)
-    upper = ((iota((SEG, SEG + LANES), 0) < ones_col) | (ones_col >= SEG)).astype(f32).astype(bf16)
-    lower = (iota((BINS, BINS), 1) < iota((BINS, BINS), 0)).astype(f32).astype(bf16)
     base = jnp.zeros((BINS, LANES), f32)
     members, counts, totals = [], [], []
     for s in range(GS // SEG):
         member = (bin_of[:, s * SEG:(s + 1) * SEG] == iota((BINS, SEG), 0)).astype(f32)
-        both = dot(member.astype(bf16), upper)
+        both = dot(member.astype(bf16), upper[...])
         members.append(member)
         counts.append(both[:, :SEG])
         totals.append(both[:, SEG:])
-        base = base + dot(lower, both[:, SEG:].astype(bf16))
+        base = base + dot(lower[...], both[:, SEG:].astype(bf16))
     places = []
     for s in range(GS // SEG):
         offset = jnp.concatenate([base] * (SEG // LANES), 1)
         places.append(jnp.sum(members[s] * (counts[s] + offset), axis=0, keepdims=True))
         base = base + totals[s]
     place = jnp.concatenate(places, 1).astype(i32)
-    slot = iota((1, GS), 1)
-    row = iota((16, GS), 0)
-    digit = jnp.where(row < 8, slot // 32, slot % 32).astype(f32)
-    left = jnp.where((place // LANES) == (row % 8), digit, 0.0).astype(bf16)
     within = jnp.where(live, place % LANES, -1)
-    right = (within == iota((LANES, GS), 0)).astype(f32).astype(bf16)
-    both = dot(left, right, ((1,), (1,)))
-    slots = (both[:8] * 32.0 + both[8:]).astype(i32)
-    return place, slots
+    to_lane = (within == iota((LANES, GS), 0)).astype(f32).astype(bf16)
+    return place, to_lane
+
+
+def in_order(values, place, to_lane):
+    n = values.shape[0]
+    first = (values * 0.99609375).astype(bf16)
+    rest = values - first.astype(f32)
+    second = rest.astype(bf16)
+    rest = rest - second.astype(f32)
+    parts = jnp.concatenate([first.astype(f32), second.astype(f32), rest] + [jnp.zeros_like(rest)] * (n // 8 % 2), 0)
+    parts = parts.astype(bf16)
+    rows = parts.shape[0]
+    chunk = jnp.broadcast_to(place // LANES, (16, GS))
+    left = []
+    for h in range(CHUNKS):
+        here = jnp.where(chunk == h, 1.0, 0.0).astype(bf16)
+        left += [parts[r:r + 16] * here for r in range(0, rows, 16)]
+    moved = dot(jnp.concatenate(left, 0), to_lane, ((1,), (1,)))
+    pieces = []
+    for h in range(CHUNKS):
+        a, b, c = (moved[h * rows + k * n:h * rows + (k + 1) * n] for k in range(3))
+        pieces.append(a + b + c)
+    return pieces
 
 
 def gather(values, index):
@@ -104,7 +118,7 @@
 def local_kernel(
     scnt_ref, tcnt_ref, before_ref, after_ref, rhs_ref, points_ref, tgt_ref,
     splace_ref, tplace_ref, w1_ref, mf_ref, mw_ref, sums_ref,
-    src_ref, rows_ref, vf_ref, vw_ref, lane_ref, tlane_ref, w2_ref, wins_v, wins_s, list_s, sem,
+    src_ref, rows_ref, vf_ref, vw_ref, lane_ref, tlane_ref, w2_ref, cache_ref, wins_v, wins_s, list_s, upper_ref, lower_ref, sem,
 ):
     own = tgt_ref.shape[1] // GS
     total = own + 2 * HALO
@@ -117,6 +131,8 @@
             src_ref[row:row + min(ref.shape[0], 11), at:at + ref.shape[1]] = ref[:11, :]
             row += ref.shape[0]
 
+    src_ref[11:16, :] = jnp.zeros((5, src_ref.shape[1]), f32)
+
     def clear(g, _):
         rows_ref[:, pl.ds(pl.multiple_of(g * ROW_STRIDE + GS, 8), WIN), :] = jnp.zeros((3, WIN, LANES), f32)
         vf_ref[:, pl.ds(pl.multiple_of(g * VAL_STRIDE + GS, LANES), 384)] = jnp.zeros((F, 384), f32)
@@ -128,42 +144,44 @@
     mf_ref[...] = jnp.zeros_like(mf_ref)
     mw_ref[...] = jnp.zeros_like(mw_ref)
 
-    def sort_source(g, _):
+    ones_col = iota((SEG, SEG + LANES), 1)
+    upper_ref[...] = ((iota((SEG, SEG + LANES), 0) < ones_col) | (ones_col >= SEG)).astype(f32).astype(bf16)
+    lower_ref[...] = (iota((BINS, BINS), 1) < iota((BINS, BINS), 0)).astype(f32).astype(bf16)
+
+    def sort_source(g):
         at = pl.multiple_of(g * GS, GS)
         live = slot_mask(scnt_ref, g)
-        count = live_total(scnt_ref, g)
-        points = jnp.concatenate([src_ref[8:11, pl.ds(at, GS)], jnp.zeros((5, GS), f32)], 0)
-        field = src_ref[0:8, pl.ds(at, GS)]
-        place, slots = order(points[1:2], live)
+        values = src_ref[:, pl.ds(at, GS)]
+        place, to_lane = order(values[9:10], live, upper_ref, lower_ref)
         splace_ref[:, pl.ds(at, GS)] = place
-        for h in range(CHUNKS):
-            index = slots[h:h + 1]
-            here = (iota((8, LANES), 1) + h * LANES) < count
-            moved = gather(points, index)
-            lane_ref[:, pl.ds(at + h * LANES, LANES)] = moved
-            wide = jnp.concatenate([moved, jnp.zeros((LANES - 8, LANES), f32)], 0)
-            wide = wide.T
+        for h, moved in enumerate(in_order(values, place, to_lane)):
+            points = moved[8:]
+            lane_ref[:, pl.ds(at + h * LANES, LANES)] = points
+            wide = jnp.concatenate([points, jnp.zeros((LANES - 8, LANES), f32)], 0).T
             row = pl.multiple_of(g * ROW_STRIDE + h * LANES, 8)
             for axis in range(3):
                 rows_ref[axis, pl.ds(row, LANES), :] = jnp.broadcast_to(wide[:, axis:axis + 1], (LANES, LANES))
-            vf_ref[:, pl.ds(pl.multiple_of(g * VAL_STRIDE + h * LANES, LANES), LANES)] = jnp.where(
-                here, gather(field, index), 0.0
-            )
-        return 0
-
-    lax.fori_loop(0, total, sort_source, 0)
-
-    def sort_target(g, _):
+            vf_ref[:, pl.ds(pl.multiple_of(g * VAL_STRIDE + h * LANES, LANES), LANES)] = moved[:8]
+
+    def sort_target(g):
         at = pl.multiple_of(g * GS, GS)
         live = slot_mask(tcnt_ref, g)
         points = jnp.concatenate([tgt_ref[:, pl.ds(at, GS)], jnp.zeros((5, GS), f32)], 0)
-        place, slots = order(points[1:2], live)
+        place, to_lane = order(points[1:2], live, upper_ref, lower_ref)
         tplace_ref[:, pl.ds(at, GS)] = place
-        for h in range(CHUNKS):
-            tlane_ref[:, pl.ds(at + h * LANES, LANES)] = gather(points, slots[h:h + 1])
-        return 0
-
-    lax.fori_loop(0, own, sort_target, 0)
+        for h, moved in enumerate(in_order(points, place, to_lane)):
+            tlane_ref[:, pl.ds(at + h * LANES, LANES)] = moved
+
+    def several(fn, n):
+        def some(i, _):
+            for u in range(TOGETHER):
+                fn(TOGETHER * i + u)
+            return 0
+
+        lax.fori_loop(0, n // TOGETHER, some, 0)
+
+    several(sort_source, total)
+    several(sort_target, own)
 
     def windows(points_ref, at, count, g, acc, column):
         place = iota((8, LANES), 1) + iota((8, LANES), 0) * LANES
@@ -185,7 +203,7 @@
             end = jnp.max(jnp.where(near, slot + 1.0, 0.0), axis=1, keepdims=True).astype(i32)
             unit = jnp.where(end > 0, first // 16, 0)
             packed = packed + unit * (128 ** b)
-            steps = jnp.maximum(steps, (end - unit * 16 + WIN - 1) // WIN)
+            steps = jnp.maximum(steps, (end - unit * 16 - WIN + MORE - 1) // MORE)
         packed = packed + steps * (128 ** 3)
         return jnp.where(iota((8, LANES), 1) == column, packed, acc)
 
@@ -203,35 +221,44 @@
     copy.start()
     copy.wait()
 
-    def interact(points, packed, k, g, value_refs):
+    def window_start(packed, b, skip):
+        return pl.multiple_of(jnp.minimum(((packed >> (7 * b)) & 127) * 16 + skip, GS), 16)
+
+    def near_phi(points, there, start, width):
+        row = pl.multiple_of(there * ROW_STRIDE + start, 16)
+        square = None
+        for axis in range(3):
+            offset = rows_ref[axis, pl.ds(row, width), :] - points[axis:axis + 1, :]
+            square = offset * offset if axis == 0 else square + offset * offset
+        square = jnp.minimum(jnp.maximum(square, 1e-30), float(R * R))
+        distance = square * lax.rsqrt(square)
+        rest = R - distance
+        rest = rest * rest
+        return jnp.concatenate(split(rest * rest * (distance + 1.0)), 1)
+
+    def near_values(value_refs, there, start, width):
+        parts = []
+        for ref in value_refs:
+            window = ref[:, pl.ds(pl.multiple_of(there * VAL_STRIDE + start // LANES * LANES, LANES), 384)]
+            window = pltpu.roll(window, lax.rem(384 - start % LANES, 384), 1)[:, :width]
+            parts += list(split(window))
+        return jnp.concatenate(parts, 0)
+
+    def interact(points, packed, skip, width, g, value_refs, keep=None, kept=None):
         acc = None
         for b in range(3):
-            there = g + b - 1
-            start = pl.multiple_of(jnp.minimum(((packed >> (7 * b)) & 127) * 16 + k * WIN, GS), 16)
-            row = pl.multiple_of(there * ROW_STRIDE + start, 16)
-            square = None
-            for axis in range(3):
-                offset = rows_ref[axis, pl.ds(row, WIN), :] - points[axis:axis + 1, :]
-                square = offset * offset if axis == 0 else square + offset * offset
-            square = jnp.minimum(jnp.maximum(square, 1e-30), float(R * R))
-            distance = square * lax.rsqrt(square)
-            rest = R - distance
-            rest = rest * rest
-            phi = rest * rest * (distance + 1.0)
-            high, low = split(phi)
-            parts = []
-            for ref in value_refs:
-                window = ref[:, pl.ds(pl.multiple_of(there * VAL_STRIDE + start // LANES * LANES, LANES), 384)]
-                window = pltpu.roll(window, lax.rem(384 - start % LANES, 384), 1)[:, :WIN]
-                parts += list(split(window))
-            left = jnp.concatenate(parts, 0)
-            term = dot(left, jnp.concatenate([high, low], 1))
+            start = window_start(packed, b, skip)
+            if kept is None:
+                phi = near_phi(points, g + b - 1, start, width)
+            else:
+                phi = cache_ref[kept, b * WIN:(b + 1) * WIN, :]
+            if keep is not None:
+                cache_ref[keep, b * WIN:(b + 1) * WIN, :] = phi
+            term = dot(near_values(value_refs, g + b - 1, start, width), phi)
             acc = term if acc is None else acc + term
         return acc[:, :LANES] + acc[:, LANES:]
 
-    def pass_over(column0, g0, groups, points_ref, cnt_ref, value_refs, store):
-        rows_out = 2 * F * len(value_refs)
-
+    def list_chunks(cnt_ref, first, end):
         def list_group(g, n):
             def list_chunk(c, n):
                 list_s[n] = g * CHUNKS + c
@@ -239,50 +266,77 @@
 
             return lax.fori_loop(0, (live_total(cnt_ref, g) + LANES - 1) // LANES, list_chunk, n)
 
-        n = lax.fori_loop(groups[0], groups[1], list_group, 0)
-
-        def batch(i, _):
-            work = []
-            for u in range(BATCH):
-                item = list_s[jnp.minimum(i * BATCH + u, n - 1)]
-                g = item // CHUNKS
-                c = item % CHUNKS
-                at = pl.multiple_of(item * LANES, LANES)
-                packed = wins_s[c, g + column0]
-                work.append((g, c, at, packed, points_ref[:, pl.ds(at, LANES)]))
-            accs = tuple(interact(points, packed, 0, g + g0, value_refs) for g, c, at, packed, points in work)
-            most = functools.reduce(jnp.maximum, [w[3] >> 21 for w in work])
-
-            def step(k, accs):
-                return tuple(
-                    acc + interact(points, packed, k, g + g0, value_refs)
-                    for acc, (g, c, at, packed, points) in zip(accs, work)
-                )
-
-            accs = lax.fori_loop(1, most, step, accs)
-            for acc, (g, c, at, packed, points) in zip(accs, work):
-                here = (iota((F, LANES), 1) + c * LANES) < live_total(cnt_ref, g)
-                for v in range(len(value_refs)):
-                    out = (acc[16 * v:16 * v + 8] + acc[16 * v + 8:16 * v + 16]) * (1.0 / 256.0)
-                    store(v, g, c, at, jnp.where(here, out, 0.0))
-            return 0
-
-        lax.fori_loop(0, (n + BATCH - 1) // BATCH, batch, 0)
+        return lax.fori_loop(first, end, list_group, 0)
+
+    def work_on(i, n, column0, g0, points_ref, cnt_ref, value_refs, store, keep=False, kept=False):
+        work = []
+        for u in range(BATCH):
+            item = list_s[jnp.minimum(i * BATCH + u, n - 1)]
+            g = item // CHUNKS
+            c = item % CHUNKS
+            at = pl.multiple_of(item * LANES, LANES)
+            packed = wins_s[c, g + column0]
+            slot = lax.rem(i, LAG + 1) * BATCH + u
+            work.append((g, c, at, packed, points_ref[:, pl.ds(at, LANES)], slot))
+        accs = tuple(
+            interact(
+                points, packed, 0, WIN, g + g0, value_refs, slot if keep else None, slot if kept else None
+            )
+            for g, c, at, packed, points, slot in work
+        )
+        for acc, (g, c, at, packed, points, slot) in zip(accs, work):
+
+            def more(k, acc, g=g, packed=packed, points=points):
+                return acc + interact(points, packed, WIN + k * MORE, MORE, g + g0, value_refs)
+
+            acc = lax.fori_loop(0, packed >> 21, more, acc)
+            here = (iota((F, LANES), 1) + c * LANES) < live_total(cnt_ref, g)
+            for v in range(len(value_refs)):
+                out = (acc[16 * v:16 * v + 8] + acc[16 * v + 8:16 * v + 16]) * (1.0 / 256.0)
+                store(v, g, c, at, jnp.where(here, out, 0.0))
 
     def store_w1(v, g, c, at, out):
         vw_ref[:, pl.ds(pl.multiple_of(g * VAL_STRIDE + c * LANES, LANES), LANES)] = out
 
-    pass_over(0, 0, (1, total - 1), lane_ref, scnt_ref, [vf_ref], store_w1)
-
     def store_w2(v, g, c, at, out):
-        w2_ref[:, pl.ds(pl.multiple_of(at - HALO * GS, LANES), LANES)] = out
-
-    pass_over(0, 0, (HALO, total - HALO), lane_ref, scnt_ref, [vw_ref], store_w2)
+        w2_ref[:, pl.ds(at, LANES)] = out
+
+    n = list_chunks(scnt_ref, 1, total - 1)
+    batches = (n + BATCH - 1) // BATCH
+
+    def first_pass(i):
+        work_on(i, n, 0, 0, lane_ref, scnt_ref, [vf_ref], store_w1, keep=True)
+
+    def second_pass(i):
+        work_on(i, n, 0, 0, lane_ref, scnt_ref, [vw_ref], store_w2, kept=True)
+
+    def lead(i, _):
+        first_pass(i)
+        return 0
+
+    def both(i, _):
+        second_pass(i - LAG)
+        first_pass(i)
+        return 0
+
+    def trail(i, _):
+        second_pass(i - LAG)
+        return 0
+
+    lax.fori_loop(0, LAG, lead, 0)
+    lax.fori_loop(LAG, batches, both, 0)
+    lax.fori_loop(jnp.maximum(batches, LAG), batches + LAG, trail, 0)
 
     def store_mapped(v, g, c, at, out):
         (mf_ref, mw_ref)[v][:, pl.ds(at, LANES)] = out
 
-    pass_over(total, HALO, (0, own), tlane_ref, tcnt_ref, [vf_ref, vw_ref], store_mapped)
+    n = list_chunks(tcnt_ref, 0, own)
+
+    def mapped_pass(i, _):
+        work_on(i, n, total, HALO, tlane_ref, tcnt_ref, [vf_ref, vw_ref], store_mapped)
+        return 0
+
+    lax.fori_loop(0, (n + BATCH - 1) // BATCH, mapped_pass, 0)
 
     def first_sums(g, acc):
         ff, fw = acc
@@ -304,7 +358,7 @@
         f = vf_ref[:, pl.ds(at, GS)]
         w = vw_ref[:, pl.ds(at, GS)]
         e = w - shift * f
-        z = w2_ref[:, pl.ds(pl.multiple_of(g * GS, GS), GS)] - shift * w
+        z = w2_ref[:, pl.ds(pl.multiple_of((g + HALO) * GS, GS), GS)] - shift * w
         return ee + e * e, ez + e * z, fz + f * z
 
     sums = lax.fori_loop(0, own, second_sums, (zero, zero, zero))
@@ -444,10 +498,13 @@
             pltpu.VMEM((F, total * VAL_STRIDE), f32),
             pltpu.VMEM((8, total * GS), f32),
             pltpu.VMEM((8, points), f32),
-            pltpu.VMEM((F, points), f32),
+            pltpu.VMEM((F, total * GS), f32),
+            pltpu.VMEM(((LAG + 1) * BATCH, 3 * WIN, 2 * LANES), bf16),
             pltpu.VMEM((8, LANES), i32),
             pltpu.SMEM((8, LANES), i32),
             pltpu.SMEM((total * CHUNKS,), i32),
+            pltpu.VMEM((SEG, SEG + LANES), bf16),
+            pltpu.VMEM((BINS, BINS), bf16),
             pltpu.SemaphoreType.DMA,
         ],
         compiler_params=pltpu.CompilerParams(vmem_limit_bytes=56 * 1024 * 1024),

time: 244 us -> 182 us (0.75)
  Pallas kernels: 232 us -> 170 us
    pallas_call x1, Pallas kernels: 198 us -> 144 us  [run_local(): pl.pallas_call(local_kernel, out_shape=[jax.ShapeDtypeStruct((1, total *...]
    pallas_call x1, Pallas kernels: 25.9 us -> 17.4 us  [run_share(): pl.pallas_call(share_kernel, out_shape=jax.ShapeDtypeStruct((F, LANES), f...]
where the time goes in v3:
time: 182 us
  Pallas kernels  170 us (93%)
  starting transfers between devices  6.43 us (4%)
  waiting for transfers between devices  1.91 us (1%)
    pallas_call x1, Pallas kernels, run_local(): pl.pallas_call(local_kernel, out_shape=[jax.ShapeDtypeStruct((1, total *...  144 us
    pallas_call x1, Pallas kernels, run_share(): pl.pallas_call(share_kernel, out_shape=jax.ShapeDtypeStruct((F, LANES), f...  17.4 us
    pallas_call x1, Pallas kernels, run_final(): pl.pallas_call(final_kernel, out_shape=[jax.ShapeDtypeStruct(arrays[0].sh...  7.85 us
    ppermute x2, starting transfers between devices, shifted(): return lax.ppermute(x, AXES, pairs)  6.43 us
  transfers between devices with their start and end apart: 2, of which 2 were waited for; matrix products, arithmetic and copies ran while one was open for 0% of the time, Pallas kernels for 0%

profile of v3, /device:TPU:1, one launch (start us, length us, event | category | flops | bytes accessed | tf_op | source)
XLA Modules:
  0.0 181.9 jit_solution(16858382458144431855)
XLA Ops:
  0.6 0.7 convert_element_type.18
  1.3 0.1 fusion.4
  1.4 0.8 fusion.3
  2.2 0.9 fusion.2
  3.1 3.3 %collective-permute-start.1 = (f32[12,2048]{1,0:T(8,128)S(1)}, f32[12,2048]{1,0:T(8,128)S(1)}, u32[]{:S(2)}, u32[]{:S(2)}) collective-permute-start(f32[12,2048]{1,0:T(8,128)S(1)} %pad_maximum_fusion.1), channel_id=1, source_target_pairs={{1,0},{2,1},{3,2},{4,3},{5,4},{6,5},{7,6},{8,7},{9,8},{10,9},{11,1... | collective-permute-start | bytes 294920 | tf_op jit(solution)/shard_map/ppermute | solution.py:554
  6.5 3.1 %collective-permute-start = (f32[12,2048]{1,0:T(8,128)S(1)}, f32[12,2048]{1,0:T(8,128)S(1)}, u32[]{:S(2)}, u32[]{:S(2)}) collective-permute-start(f32[12,2048]{1,0:T(8,128)S(1)} %pad_maximum_fusion), channel_id=1, source_target_pairs={{0,1},{1,2},{2,3},{3,4},{4,5},{5,6},{6,7},{7,8},{8,9},{9,10},{10,1... | collective-permute-start | bytes 294920 | tf_op jit(solution)/shard_map/ppermute | solution.py:554
  9.6 0.7 collective-permute-done.1.after_ref
  10.2 0.0 copy-start
  10.2 0.0 copy-start.2
  10.3 1.2 collective-permute-done.before_ref
  11.5 0.0 copy-start.1
  11.5 0.0 copy-done.2
  11.5 0.6 pad_add_fusion.scnt_ref
  12.1 0.0 copy-done
  12.2 0.0 copy-done.1
  12.2 144.3 %local.1 = (s32[1,20480]{1,0:T(1,128)}, s32[1,16384]{1,0:T(1,128)}, f32[8,16384]{1,0:T(8,128)}, f32[8,16384]{1,0:T(8,128)}, f32[8,16384]{1,0:T(8,128)}, /*index=5*/f32[8,128]{1,0:T(8,128)}) custom-call(s32[80]{0:T(128)} %pad_add_fusion.scnt_ref, s32[64]{0:T(128)} %tcnt_ref.3, f32[12,2048]{1,0:T(8,128)} %copy-done.1, f32[12,2048]{1,0:T(8,128)} %copy-done, ...), custom_call_target="tpu_custom_call" | custom-call | tf_op jit(solution)/shard_map/local/pallas_call | solution.py:482
  156.5 17.4 %share.1.scale_ref = f32[8,128]{1,0:T(8,128)} custom-call(f32[8,128]{1,0:T(8,128)} %get-tuple-element.8.sums_ref), custom_call_target="tpu_custom_call" | custom-call | tf_op jit(solution)/shard_map/share/pallas_call | solution.py:517
  173.9 7.8 %final.1 = (f32[8,16384]{1,0:T(8,128)}, f32[8,16384]{1,0:T(8,128)}) custom-call(s32[64]{0:T(128)} %scnt_ref.1, s32[64]{0:T(128)} %tcnt_ref.3, f32[8,128]{1,0:T(8,128)} %share.1.scale_ref, f32[8,16384]{1,0:T(8,128)} %rhs_hbm.1, s32[1,20480]{1,0:T(1,128)} %get-tuple-element.9.splace_hbm, s32[1,16384]{1,0:T(1,128)} %get-tuple-element.10.tplace_hbm, ...), custom_call_target="tpu_custom_call" | custom-call | tf_op jit(solution)/shard_map/final/pallas_call | solution.py:539
  (6 shorter events, 0.1 us)
Async XLA Ops:
  3.1 7.2 %collective-permute-start.1 = (f32[12,2048]{1,0:T(8,128)S(1)}, f32[12,2048]{1,0:T(8,128)S(1)}, u32[]{:S(2)}, u32[]{:S(2)}) collective-permute-start(f32[12,2048]{1,0:T(8,128)S(1)} %pad_maximum_fusion.1), channel_id=1, source_target_pairs={{1,0},{2,1},{3,2},{4,3},{5,4},{6,5},{7,6},{8,7},{9,8},{10,9},{11,1... | collective-permute-start | bytes 294920 | tf_op jit(solution)/shard_map/ppermute | solution.py:554
  6.5 5.0 %collective-permute-start = (f32[12,2048]{1,0:T(8,128)S(1)}, f32[12,2048]{1,0:T(8,128)S(1)}, u32[]{:S(2)}, u32[]{:S(2)}) collective-permute-start(f32[12,2048]{1,0:T(8,128)S(1)} %pad_maximum_fusion), channel_id=1, source_target_pairs={{0,1},{1,2},{2,3},{3,4},{4,5},{5,6},{6,7},{7,8},{8,9},{9,10},{10,1... | collective-permute-start | bytes 294920 | tf_op jit(solution)/shard_map/ppermute | solution.py:554
  10.2 1.9 %copy-start = (f32[12,2048]{1,0:T(8,128)}, f32[12,2048]{1,0:T(8,128)S(1)}, u32[]{:S(2)}) copy-start(f32[12,2048]{1,0:T(8,128)S(1)} %collective-permute-done.1.after_ref) | copy-start | bytes 294916
  10.2 1.3 copy-start.2
  11.5 0.7 copy-start.1

commit v4 on v3

--- a/solution.py
+++ b/solution.py
@@ -13,9 +13,11 @@
 LANES = 128
 CHUNKS = GS // LANES
 BINS = 128
-WIN = 192
+WINS = (208, 176, 208)
+WIN_AT = (0, 208, 384)
 MORE = 64
-ROW_STRIDE = GS + WIN
+PIECE = 16
+ROW_STRIDE = GS + max(WINS)
 VAL_STRIDE = GS + 384
 SEG = 256
 BATCH = 4
@@ -57,34 +59,35 @@
     scale = BINS / jnp.maximum(high - low, 1e-30)
     scaled = jnp.minimum(jnp.maximum((y - low) * scale, 0.0), BINS - 1.0)
     bin_of = jnp.where(live, scaled.astype(i32), BINS)
-    base = jnp.zeros((BINS, LANES), f32)
-    members, counts, totals = [], [], []
+    members, counts = [], []
     for s in range(GS // SEG):
         member = (bin_of[:, s * SEG:(s + 1) * SEG] == iota((BINS, SEG), 0)).astype(f32)
-        both = dot(member.astype(bf16), upper[...])
         members.append(member)
-        counts.append(both[:, :SEG])
-        totals.append(both[:, SEG:])
-        base = base + dot(lower[...], both[:, SEG:].astype(bf16))
+        counts.append(dot(member.astype(bf16), upper[...]))
+    totals = [c[:, -1:] + m[:, -1:] for c, m in zip(counts, members)]
+    column = iota((BINS, LANES), 1)
+    table = jnp.zeros((BINS, LANES), f32)
+    for s, t in enumerate(totals):
+        table = jnp.where(column == s, t, table)
+    base = jnp.sum(dot(lower[...], table.astype(bf16)), axis=1, keepdims=True)
     places = []
-    for s in range(GS // SEG):
-        offset = jnp.concatenate([base] * (SEG // LANES), 1)
-        places.append(jnp.sum(members[s] * (counts[s] + offset), axis=0, keepdims=True))
-        base = base + totals[s]
+    for m, c, t in zip(members, counts, totals):
+        places.append(jnp.sum(m * (c + base), axis=0, keepdims=True))
+        base = base + t
     place = jnp.concatenate(places, 1).astype(i32)
     within = jnp.where(live, place % LANES, -1)
     to_lane = (within == iota((LANES, GS), 0)).astype(f32).astype(bf16)
     return place, to_lane
 
 
-def in_order(values, place, to_lane):
-    n = values.shape[0]
-    first = (values * 0.99609375).astype(bf16)
-    rest = values - first.astype(f32)
-    second = rest.astype(bf16)
-    rest = rest - second.astype(f32)
-    parts = jnp.concatenate([first.astype(f32), second.astype(f32), rest] + [jnp.zeros_like(rest)] * (n // 8 % 2), 0)
-    parts = parts.astype(bf16)
+def in_order(points, field, place, to_lane):
+    first = (points * 0.99609375).astype(bf16).astype(f32)
+    second = (points - first).astype(bf16).astype(f32)
+    parts = [first, second, points - first - second, jnp.zeros((7, GS), f32)]
+    if field is not None:
+        high = field.astype(bf16).astype(f32)
+        parts += [high, field - high]
+    parts = jnp.concatenate(parts, 0).astype(bf16)
     rows = parts.shape[0]
     chunk = jnp.broadcast_to(place // LANES, (16, GS))
     left = []
@@ -94,8 +97,10 @@
     moved = dot(jnp.concatenate(left, 0), to_lane, ((1,), (1,)))
     pieces = []
     for h in range(CHUNKS):
-        a, b, c = (moved[h * rows + k * n:h * rows + (k + 1) * n] for k in range(3))
-        pieces.append(a + b + c)
+        piece = moved[h * rows:(h + 1) * rows]
+        points = piece[0:3] + piece[3:6] + piece[6:9]
+        points = jnp.concatenate([points, jnp.zeros((5, LANES), f32)], 0)
+        pieces.append((points, None if field is None else piece[16:24] + piece[24:32], piece[:16]))
     return pieces
 
 
@@ -118,7 +123,7 @@
 def local_kernel(
     scnt_ref, tcnt_ref, before_ref, after_ref, rhs_ref, points_ref, tgt_ref,
     splace_ref, tplace_ref, w1_ref, mf_ref, mw_ref, sums_ref,
-    src_ref, rows_ref, vf_ref, vw_ref, lane_ref, tlane_ref, w2_ref, cache_ref, wins_v, wins_s, list_s, upper_ref, lower_ref, sem,
+    src_ref, rows_ref, vf_ref, vw_ref, lane_ref, tlane_ref, w2_ref, cache_ref, wins_v, wins_s, list_s, upper_ref, lower_ref, spread_ref, sem,
 ):
     own = tgt_ref.shape[1] // GS
     total = own + 2 * HALO
@@ -134,7 +139,9 @@
     src_ref[11:16, :] = jnp.zeros((5, src_ref.shape[1]), f32)
 
     def clear(g, _):
-        rows_ref[:, pl.ds(pl.multiple_of(g * ROW_STRIDE + GS, 8), WIN), :] = jnp.zeros((3, WIN, LANES), f32)
+        rows_ref[:, pl.ds(pl.multiple_of(g * ROW_STRIDE + GS, 8), max(WINS)), :] = jnp.zeros(
+            (3, max(WINS), LANES), f32
+        )
         vf_ref[:, pl.ds(pl.multiple_of(g * VAL_STRIDE + GS, LANES), 384)] = jnp.zeros((F, 384), f32)
         vw_ref[:, pl.ds(pl.multiple_of(g * VAL_STRIDE, LANES), VAL_STRIDE)] = jnp.zeros((F, VAL_STRIDE), f32)
         return 0
@@ -144,9 +151,11 @@
     mf_ref[...] = jnp.zeros_like(mf_ref)
     mw_ref[...] = jnp.zeros_like(mw_ref)
 
-    ones_col = iota((SEG, SEG + LANES), 1)
-    upper_ref[...] = ((iota((SEG, SEG + LANES), 0) < ones_col) | (ones_col >= SEG)).astype(f32).astype(bf16)
+    upper_ref[...] = (iota((SEG, SEG), 0) < iota((SEG, SEG), 1)).astype(f32).astype(bf16)
     lower_ref[...] = (iota((BINS, BINS), 1) < iota((BINS, BINS), 0)).astype(f32).astype(bf16)
+
+    part = iota((16, 3 * LANES), 0)
+    spread_ref[...] = ((part < 9) & (part % 3 == iota((16, 3 * LANES), 1) // LANES)).astype(f32).astype(bf16)
 
     def sort_source(g):
         at = pl.multiple_of(g * GS, GS)
@@ -154,22 +163,22 @@
         values = src_ref[:, pl.ds(at, GS)]
         place, to_lane = order(values[9:10], live, upper_ref, lower_ref)
         splace_ref[:, pl.ds(at, GS)] = place
-        for h, moved in enumerate(in_order(values, place, to_lane)):
-            points = moved[8:]
+        pieces = in_order(values[8:11], values[:8], place, to_lane)
+        for h, (points, field, _) in enumerate(pieces):
             lane_ref[:, pl.ds(at + h * LANES, LANES)] = points
-            wide = jnp.concatenate([points, jnp.zeros((LANES - 8, LANES), f32)], 0).T
-            row = pl.multiple_of(g * ROW_STRIDE + h * LANES, 8)
-            for axis in range(3):
-                rows_ref[axis, pl.ds(row, LANES), :] = jnp.broadcast_to(wide[:, axis:axis + 1], (LANES, LANES))
-            vf_ref[:, pl.ds(pl.multiple_of(g * VAL_STRIDE + h * LANES, LANES), LANES)] = moved[:8]
+            vf_ref[:, pl.ds(pl.multiple_of(g * VAL_STRIDE + h * LANES, LANES), LANES)] = field
+        parts = jnp.concatenate([piece[2] for piece in pieces], 1).astype(bf16)
+        wide = dot(parts, spread_ref[...], ((0,), (0,)))
+        for axis in range(3):
+            rows_ref[axis, pl.ds(pl.multiple_of(g * ROW_STRIDE, 8), GS), :] = wide[:, axis * LANES:(axis + 1) * LANES]
 
     def sort_target(g):
         at = pl.multiple_of(g * GS, GS)
         live = slot_mask(tcnt_ref, g)
-        points = jnp.concatenate([tgt_ref[:, pl.ds(at, GS)], jnp.zeros((5, GS), f32)], 0)
+        points = tgt_ref[:, pl.ds(at, GS)]
         place, to_lane = order(points[1:2], live, upper_ref, lower_ref)
         tplace_ref[:, pl.ds(at, GS)] = place
-        for h, moved in enumerate(in_order(points, place, to_lane)):
+        for h, (moved, _, _) in enumerate(in_order(points, None, place, to_lane)):
             tlane_ref[:, pl.ds(at + h * LANES, LANES)] = moved
 
     def several(fn, n):
@@ -201,9 +210,9 @@
             slot = slot.astype(f32)
             first = jnp.min(jnp.where(near, slot, 4096.0), axis=1, keepdims=True).astype(i32)
             end = jnp.max(jnp.where(near, slot + 1.0, 0.0), axis=1, keepdims=True).astype(i32)
-            unit = jnp.where(end > 0, first // 16, 0)
+            unit = jnp.where(end > 0, first // 8, 0)
             packed = packed + unit * (128 ** b)
-            steps = jnp.maximum(steps, (end - unit * 16 - WIN + MORE - 1) // MORE)
+            steps = jnp.maximum(steps, (end - unit * 8 - WINS[b] + MORE - 1) // MORE)
         packed = packed + steps * (128 ** 3)
         return jnp.where(iota((8, LANES), 1) == column, packed, acc)
 
@@ -215,26 +224,32 @@
             tlane_ref, pl.multiple_of(g * GS, GS), live_total(tcnt_ref, g), g + HALO, acc, g + total
         )
 
-    acc = lax.fori_loop(1, total - 1, source_windows, jnp.zeros((8, LANES), i32))
-    wins_v[...] = lax.fori_loop(0, own, target_windows, acc)
+    def two(fn, first):
+        return lambda i, acc: fn(first + 2 * i + 1, fn(first + 2 * i, acc))
+
+    acc = lax.fori_loop(0, (total - 2) // 2, two(source_windows, 1), jnp.zeros((8, LANES), i32))
+    wins_v[...] = lax.fori_loop(0, own // 2, two(target_windows, 0), acc)
     copy = pltpu.make_async_copy(wins_v, wins_s, sem)
     copy.start()
     copy.wait()
 
     def window_start(packed, b, skip):
-        return pl.multiple_of(jnp.minimum(((packed >> (7 * b)) & 127) * 16 + skip, GS), 16)
+        return pl.multiple_of(jnp.minimum(((packed >> (7 * b)) & 127) * 8 + skip, GS), 8)
 
     def near_phi(points, there, start, width):
-        row = pl.multiple_of(there * ROW_STRIDE + start, 16)
-        square = None
-        for axis in range(3):
-            offset = rows_ref[axis, pl.ds(row, width), :] - points[axis:axis + 1, :]
-            square = offset * offset if axis == 0 else square + offset * offset
-        square = jnp.minimum(jnp.maximum(square, 1e-30), float(R * R))
-        distance = square * lax.rsqrt(square)
-        rest = R - distance
-        rest = rest * rest
-        return jnp.concatenate(split(rest * rest * (distance + 1.0)), 1)
+        row = pl.multiple_of(there * ROW_STRIDE + start, 8)
+        pieces = []
+        for r in range(0, width, PIECE):
+            square = None
+            for axis in range(3):
+                offset = rows_ref[axis, pl.ds(row + r, PIECE), :] - points[axis:axis + 1, :]
+                square = offset * offset if axis == 0 else square + offset * offset
+            square = jnp.minimum(jnp.maximum(square, 1e-30), float(R * R))
+            distance = square * lax.rsqrt(square)
+            rest = R - distance
+            rest = rest * rest
+            pieces.append(jnp.concatenate(split(rest * rest * (distance + 1.0)), 1))
+        return jnp.concatenate(pieces, 0)
 
     def near_values(value_refs, there, start, width):
         parts = []
@@ -244,16 +259,18 @@
             parts += list(split(window))
         return jnp.concatenate(parts, 0)
 
-    def interact(points, packed, skip, width, g, value_refs, keep=None, kept=None):
+    def interact(points, packed, skips, widths, g, value_refs, keep=None, kept=None):
         acc = None
         for b in range(3):
-            start = window_start(packed, b, skip)
+            width = widths[b]
+            start = window_start(packed, b, skips[b])
+            rows = slice(WIN_AT[b], WIN_AT[b] + width)
             if kept is None:
                 phi = near_phi(points, g + b - 1, start, width)
             else:
-                phi = cache_ref[kept, b * WIN:(b + 1) * WIN, :]
+                phi = cache_ref[kept, rows, :]
             if keep is not None:
-                cache_ref[keep, b * WIN:(b + 1) * WIN, :] = phi
+                cache_ref[keep, rows, :] = phi
             term = dot(near_values(value_refs, g + b - 1, start, width), phi)
             acc = term if acc is None else acc + term
         return acc[:, :LANES] + acc[:, LANES:]
@@ -268,7 +285,7 @@
 
         return lax.fori_loop(first, end, list_group, 0)
 
-    def work_on(i, n, column0, g0, points_ref, cnt_ref, value_refs, store, keep=False, kept=False):
+    def work_on(i, n, column0, g0, points_ref, cnt_ref, value_refs, place, keep=False, kept=False):
         work = []
         for u in range(BATCH):
             item = list_s[jnp.minimum(i * BATCH + u, n - 1)]
@@ -277,63 +294,82 @@
             at = pl.multiple_of(item * LANES, LANES)
             packed = wins_s[c, g + column0]
             slot = lax.rem(i, LAG + 1) * BATCH + u
-            work.append((g, c, at, packed, points_ref[:, pl.ds(at, LANES)], slot))
+            steps = jnp.where(i * BATCH + u < n, packed >> 21, 0)
+            work.append((g, c, at, packed, points_ref[:, pl.ds(at, LANES)], slot, steps))
         accs = tuple(
             interact(
-                points, packed, 0, WIN, g + g0, value_refs, slot if keep else None, slot if kept else None
+                points, packed, (0, 0, 0), WINS, g + g0, value_refs, slot if keep else None, slot if kept else None
             )
-            for g, c, at, packed, points, slot in work
+            for g, c, at, packed, points, slot, steps in work
         )
-        for acc, (g, c, at, packed, points, slot) in zip(accs, work):
-
-            def more(k, acc, g=g, packed=packed, points=points):
-                return acc + interact(points, packed, WIN + k * MORE, MORE, g + g0, value_refs)
-
-            acc = lax.fori_loop(0, packed >> 21, more, acc)
+
+        def finish(acc, v, g, c):
             here = (iota((F, LANES), 1) + c * LANES) < live_total(cnt_ref, g)
+            out = (acc[16 * v:16 * v + 8] + acc[16 * v + 8:16 * v + 16]) * (1.0 / 256.0)
+            return jnp.where(here, out, 0.0)
+
+        for acc, (g, c, at, packed, points, slot, steps) in zip(accs, work):
             for v in range(len(value_refs)):
-                out = (acc[16 * v:16 * v + 8] + acc[16 * v + 8:16 * v + 16]) * (1.0 / 256.0)
-                store(v, g, c, at, jnp.where(here, out, 0.0))
-
-    def store_w1(v, g, c, at, out):
-        vw_ref[:, pl.ds(pl.multiple_of(g * VAL_STRIDE + c * LANES, LANES), LANES)] = out
-
-    def store_w2(v, g, c, at, out):
-        w2_ref[:, pl.ds(at, LANES)] = out
+                place(v, g, c, at)[...] = finish(acc, v, g, c)
+
+        def rest():
+            for g, c, at, packed, points, slot, steps in work:
+
+                def more(k, _, g=g, c=c, at=at, packed=packed, points=points):
+                    skips = [w + k * MORE for w in WINS]
+                    acc = interact(points, packed, skips, (MORE,) * 3, g + g0, value_refs)
+                    for v in range(len(value_refs)):
+                        place(v, g, c, at)[...] += finish(acc, v, g, c)
+                    return 0
+
+                lax.fori_loop(0, steps, more, 0)
+
+        return sum(w[-1] for w in work), rest
+
+    def run_rest(*rests):
+        @pl.when(sum(steps for steps, _ in rests) > 0)
+        def _():
+            for _, rest in rests:
+                rest()
+
+    def place_w1(v, g, c, at):
+        return vw_ref.at[:, pl.ds(pl.multiple_of(g * VAL_STRIDE + c * LANES, LANES), LANES)]
+
+    def place_w2(v, g, c, at):
+        return w2_ref.at[:, pl.ds(at, LANES)]
 
     n = list_chunks(scnt_ref, 1, total - 1)
     batches = (n + BATCH - 1) // BATCH
 
     def first_pass(i):
-        work_on(i, n, 0, 0, lane_ref, scnt_ref, [vf_ref], store_w1, keep=True)
+        return work_on(i, n, 0, 0, lane_ref, scnt_ref, [vf_ref], place_w1, keep=True)
 
     def second_pass(i):
-        work_on(i, n, 0, 0, lane_ref, scnt_ref, [vw_ref], store_w2, kept=True)
+        return work_on(i, n, 0, 0, lane_ref, scnt_ref, [vw_ref], place_w2, kept=True)
 
     def lead(i, _):
-        first_pass(i)
+        run_rest(first_pass(i))
         return 0
 
     def both(i, _):
-        second_pass(i - LAG)
-        first_pass(i)
+        run_rest(second_pass(i - LAG), first_pass(i))
         return 0
 
     def trail(i, _):
-        second_pass(i - LAG)
+        run_rest(second_pass(i - LAG))
         return 0
 
     lax.fori_loop(0, LAG, lead, 0)
     lax.fori_loop(LAG, batches, both, 0)
     lax.fori_loop(jnp.maximum(batches, LAG), batches + LAG, trail, 0)
 
-    def store_mapped(v, g, c, at, out):
-        (mf_ref, mw_ref)[v][:, pl.ds(at, LANES)] = out
+    def place_mapped(v, g, c, at):
+        return (mf_ref, mw_ref)[v].at[:, pl.ds(at, LANES)]
 
     n = list_chunks(tcnt_ref, 0, own)
 
     def mapped_pass(i, _):
-        work_on(i, n, total, HALO, tlane_ref, tcnt_ref, [vf_ref, vw_ref], store_mapped)
+        run_rest(work_on(i, n, total, HALO, tlane_ref, tcnt_ref, [vf_ref, vw_ref], place_mapped))
         return 0
 
     lax.fori_loop(0, (n + BATCH - 1) // BATCH, mapped_pass, 0)
@@ -499,12 +535,13 @@
             pltpu.VMEM((8, total * GS), f32),
             pltpu.VMEM((8, points), f32),
             pltpu.VMEM((F, total * GS), f32),
-            pltpu.VMEM(((LAG + 1) * BATCH, 3 * WIN, 2 * LANES), bf16),
+            pltpu.VMEM(((LAG + 1) * BATCH, sum(WINS), 2 * LANES), bf16),
             pltpu.VMEM((8, LANES), i32),
             pltpu.SMEM((8, LANES), i32),
             pltpu.SMEM((total * CHUNKS,), i32),
-            pltpu.VMEM((SEG, SEG + LANES), bf16),
+            pltpu.VMEM((SEG, SEG), bf16),
             pltpu.VMEM((BINS, BINS), bf16),
+            pltpu.VMEM((16, 3 * LANES), bf16),
             pltpu.SemaphoreType.DMA,
         ],
         compiler_params=pltpu.CompilerParams(vmem_limit_bytes=56 * 1024 * 1024),

time: 182 us -> 164 us (0.901)
  Pallas kernels: 170 us -> 152 us
    pallas_call x1, Pallas kernels: 144 us -> 121 us  [run_local(): pl.pallas_call(local_kernel, out_shape=[jax.ShapeDtypeStruct((1, total *...]
    pallas_call x1, Pallas kernels: 17.4 us -> 22.4 us  [run_share(): pl.pallas_call(share_kernel, out_shape=jax.ShapeDtypeStruct((F, LANES), f...]
where the time goes in v4:
time: 164 us
  Pallas kernels  152 us (93%)
  starting transfers between devices  6.43 us (4%)
  waiting for transfers between devices  1.91 us (1%)
  local copies, waits for them, and re-layouts  1.77 us (1%)
    pallas_call x1, Pallas kernels, run_local(): pl.pallas_call(local_kernel, out_shape=[jax.ShapeDtypeStruct((1, total *...  121 us
    pallas_call x1, Pallas kernels, run_share(): pl.pallas_call(share_kernel, out_shape=jax.ShapeDtypeStruct((F, LANES), f...  22.4 us
    pallas_call x1, Pallas kernels, run_final(): pl.pallas_call(final_kernel, out_shape=[jax.ShapeDtypeStruct(arrays[0].sh...  7.85 us
    ppermute x2, starting transfers between devices, shifted(): return lax.ppermute(x, AXES, pairs)  6.43 us
  transfers between devices with their start and end apart: 2, of which 2 were waited for; matrix products, arithmetic and copies ran while one was open for 0% of the time, Pallas kernels for 0%

profile of v4, /device:TPU:1, one launch (start us, length us, event | category | flops | bytes accessed | tf_op | source)
XLA Modules:
  0.0 163.9 jit_solution(382621782237092875)
XLA Ops:
  0.6 0.7 convert_element_type.18
  1.3 0.1 fusion.4
  1.4 0.8 fusion.3
  2.2 0.9 fusion.2
  3.1 3.3 %collective-permute-start.1 = (f32[12,2048]{1,0:T(8,128)S(1)}, f32[12,2048]{1,0:T(8,128)S(1)}, u32[]{:S(2)}, u32[]{:S(2)}) collective-permute-start(f32[12,2048]{1,0:T(8,128)S(1)} %pad_maximum_fusion.1), channel_id=1, source_target_pairs={{1,0},{2,1},{3,2},{4,3},{5,4},{6,5},{7,6},{8,7},{9,8},{10,9},{11,1... | collective-permute-start | bytes 294920 | tf_op jit(solution)/shard_map/ppermute | solution.py:591
  6.5 3.1 %collective-permute-start = (f32[12,2048]{1,0:T(8,128)S(1)}, f32[12,2048]{1,0:T(8,128)S(1)}, u32[]{:S(2)}, u32[]{:S(2)}) collective-permute-start(f32[12,2048]{1,0:T(8,128)S(1)} %pad_maximum_fusion), channel_id=1, source_target_pairs={{0,1},{1,2},{2,3},{3,4},{4,5},{5,6},{6,7},{7,8},{8,9},{9,10},{10,1... | collective-permute-start | bytes 294920 | tf_op jit(solution)/shard_map/ppermute | solution.py:591
  9.6 0.7 collective-permute-done.1.after_ref
  10.2 0.0 copy-start
  10.2 0.0 copy-start.2
  10.3 1.2 collective-permute-done.before_ref
  11.5 0.0 copy-start.1
  11.5 0.0 copy-done.2
  11.5 0.6 pad_add_fusion.scnt_ref
  12.1 0.0 copy-done
  12.2 0.0 copy-done.1
  12.2 121.5 %local.1 = (s32[1,20480]{1,0:T(1,128)}, s32[1,16384]{1,0:T(1,128)}, f32[8,16384]{1,0:T(8,128)}, f32[8,16384]{1,0:T(8,128)}, f32[8,16384]{1,0:T(8,128)}, /*index=5*/f32[8,128]{1,0:T(8,128)}) custom-call(s32[80]{0:T(128)} %pad_add_fusion.scnt_ref, s32[64]{0:T(128)} %tcnt_ref.3, f32[12,2048]{1,0:T(8,128)} %copy-done.1, f32[12,2048]{1,0:T(8,128)} %copy-done, ...), custom_call_target="tpu_custom_call" | custom-call | tf_op jit(solution)/shard_map/local/pallas_call | solution.py:518
  133.6 22.4 %share.1.scale_ref = f32[8,128]{1,0:T(8,128)} custom-call(f32[8,128]{1,0:T(8,128)} %get-tuple-element.8.sums_ref), custom_call_target="tpu_custom_call" | custom-call | tf_op jit(solution)/shard_map/share/pallas_call | solution.py:554
  156.1 7.8 %final.1 = (f32[8,16384]{1,0:T(8,128)}, f32[8,16384]{1,0:T(8,128)}) custom-call(s32[64]{0:T(128)} %scnt_ref.1, s32[64]{0:T(128)} %tcnt_ref.3, f32[8,128]{1,0:T(8,128)} %share.1.scale_ref, f32[8,16384]{1,0:T(8,128)} %rhs_hbm.1, s32[1,20480]{1,0:T(1,128)} %get-tuple-element.9.splace_hbm, s32[1,16384]{1,0:T(1,128)} %get-tuple-element.10.tplace_hbm, ...), custom_call_target="tpu_custom_call" | custom-call | tf_op jit(solution)/shard_map/final/pallas_call | solution.py:576
  (6 shorter events, 0.1 us)
Async XLA Ops:
  3.1 7.2 %collective-permute-start.1 = (f32[12,2048]{1,0:T(8,128)S(1)}, f32[12,2048]{1,0:T(8,128)S(1)}, u32[]{:S(2)}, u32[]{:S(2)}) collective-permute-start(f32[12,2048]{1,0:T(8,128)S(1)} %pad_maximum_fusion.1), channel_id=1, source_target_pairs={{1,0},{2,1},{3,2},{4,3},{5,4},{6,5},{7,6},{8,7},{9,8},{10,9},{11,1... | collective-permute-start | bytes 294920 | tf_op jit(solution)/shard_map/ppermute | solution.py:591
  6.5 5.0 %collective-permute-start = (f32[12,2048]{1,0:T(8,128)S(1)}, f32[12,2048]{1,0:T(8,128)S(1)}, u32[]{:S(2)}, u32[]{:S(2)}) collective-permute-start(f32[12,2048]{1,0:T(8,128)S(1)} %pad_maximum_fusion), channel_id=1, source_target_pairs={{0,1},{1,2},{2,3},{3,4},{4,5},{5,6},{6,7},{7,8},{8,9},{9,10},{10,1... | collective-permute-start | bytes 294920 | tf_op jit(solution)/shard_map/ppermute | solution.py:591
  10.2 1.9 %copy-start = (f32[12,2048]{1,0:T(8,128)}, f32[12,2048]{1,0:T(8,128)S(1)}, u32[]{:S(2)}) copy-start(f32[12,2048]{1,0:T(8,128)S(1)} %collective-permute-done.1.after_ref) | copy-start | bytes 294916
  10.2 1.3 copy-start.2
  11.5 0.7 copy-start.1

commit v5 on v4

--- a/solution.py
+++ b/solution.py
@@ -121,7 +121,7 @@
 
 
 def local_kernel(
-    scnt_ref, tcnt_ref, before_ref, after_ref, rhs_ref, points_ref, tgt_ref,
+    scnt_ref, tcnt_ref, bf_ref, bx_ref, af_ref, ax_ref, rhs_ref, points_ref, tgt_ref,
     splace_ref, tplace_ref, w1_ref, mf_ref, mw_ref, sums_ref,
     src_ref, rows_ref, vf_ref, vw_ref, lane_ref, tlane_ref, w2_ref, cache_ref, wins_v, wins_s, list_s, upper_ref, lower_ref, spread_ref, sem,
 ):
@@ -130,12 +130,9 @@
 
     reach = HALO * GS
     points = tgt_ref.shape[1]
-    for at, refs in ((0, (before_ref,)), (reach, (rhs_ref, points_ref)), (reach + points, (after_ref,))):
-        row = 0
-        for ref in refs:
-            src_ref[row:row + min(ref.shape[0], 11), at:at + ref.shape[1]] = ref[:11, :]
-            row += ref.shape[0]
-
+    for at, field, coords in ((0, bf_ref, bx_ref), (reach, rhs_ref, points_ref), (reach + points, af_ref, ax_ref)):
+        src_ref[0:8, at:at + field.shape[1]] = field[...]
+        src_ref[8:11, at:at + field.shape[1]] = coords[...]
     src_ref[11:16, :] = jnp.zeros((5, src_ref.shape[1]), f32)
 
     def clear(g, _):
@@ -424,9 +421,15 @@
     ]
 
 
-def share_kernel(sums_ref, out_ref, first, second, send1, recv1, send2, recv2):
+def finish_kernel(
+    scnt_ref, tcnt_ref, sums_ref, rhs_hbm, splace_hbm, tplace_hbm, w1_hbm, mf_hbm, mw_hbm,
+    coef_ref, mapped_ref,
+    rhs_ref, splace_ref, tplace_ref, w1_ref, mf_ref, mw_ref,
+    first, second, local, send1, recv1, send2, recv2,
+):
     me = [lax.axis_index(name) for name in AXES]
     sizes = (second.shape[0], first.shape[0])
+    own = rhs_ref.shape[1] // GS
 
     def peer(axis, by):
         return {AXES[axis]: lax.rem(me[axis] + by, sizes[axis])}
@@ -437,6 +440,15 @@
             pl.semaphore_signal(
                 barrier, inc=1, device_id=peer(axis, by), device_id_type=pl.DeviceIdType.MESH
             )
+    loads = [
+        pltpu.make_async_copy(here, there, local.at[n])
+        for n, (here, there) in enumerate([
+            (rhs_hbm, rhs_ref), (splace_hbm, splace_ref), (tplace_hbm, tplace_ref),
+            (w1_hbm, w1_ref), (mf_hbm, mf_ref), (mw_hbm, mw_ref),
+        ])
+    ]
+    for load in loads:
+        load.start()
     pl.semaphore_wait(barrier, sizes[0] + sizes[1] - 2)
 
     def exchange(axis, slots, send, recv):
@@ -452,14 +464,37 @@
             )
             copy.start()
             copies.append(copy)
-        for copy in copies:
-            copy.wait()
+        return copies
+
+    def restore(g, _):
+        at = pl.multiple_of(g * GS, GS)
+        w, f, m = (ref[:, pl.ds(at, GS)] for ref in (w1_ref, mf_ref, mw_ref))
+        splace = splace_ref[:, pl.ds(pl.multiple_of(at + HALO * GS, GS), GS)]
+        tplace = tplace_ref[:, pl.ds(at, GS)]
+        slive = slot_mask(scnt_ref, g)
+        tlive = slot_mask(tcnt_ref, g)
+        for h in range(CHUNKS):
+            lanes = slice(h * LANES, (h + 1) * LANES)
+            to = pl.ds(at + h * LANES, LANES)
+            rhs_ref[:, to] = jnp.where(slive[:, lanes], rhs_ref[:, to], 0.0)
+            w1_ref[:, to] = jnp.where(slive[:, lanes], gather(w, splace[:, lanes]), 0.0)
+            mf_ref[:, to] = jnp.where(tlive[:, lanes], gather(f, tplace[:, lanes]), 0.0)
+            mw_ref[:, to] = jnp.where(tlive[:, lanes], gather(m, tplace[:, lanes]), 0.0)
+        return 0
 
     first[0] = sums_ref[...]
-    exchange(1, first, send1, recv1)
+    copies = exchange(1, first, send1, recv1)
+    for load in loads:
+        load.wait()
+    lax.fori_loop(0, own // 4, restore, 0)
+    for copy in copies:
+        copy.wait()
     part = merge(first[...])
     second[0] = jnp.concatenate(part + [jnp.zeros((3, LANES), f32)], 0)
-    exchange(0, second, send2, recv2)
+    copies = exchange(0, second, send2, recv2)
+    lax.fori_loop(own // 4, own, restore, 0)
+    for copy in copies:
+        copy.wait()
     total, mean, e_e, e_ae, _ = merge(second[...])
     alpha0 = 1.0 / mean
     ratio = e_e / total
@@ -467,47 +502,17 @@
     alpha1 = e_e / (e_ae - alpha0 * ratio * e_e)
     c1 = -alpha1 * alpha0
     c0 = alpha0 + alpha1 * (1.0 + beta)
-    out_ref[...] = jnp.concatenate([c0, c1, jnp.zeros((LANES - 2, LANES), f32)], 0).T[:F]
-
-
-def final_kernel(
-    scnt_ref, tcnt_ref, scale_ref, rhs_hbm, splace_hbm, tplace_hbm, w1_hbm, mf_hbm, mw_hbm,
-    coef_ref, mapped_ref,
-    rhs_ref, splace_ref, tplace_ref, w1_ref, mf_ref, mw_ref, sems,
-):
-    copies = [
-        pltpu.make_async_copy(here, there, sems.at[n])
-        for n, (here, there) in enumerate([
-            (rhs_hbm, rhs_ref), (splace_hbm, splace_ref), (tplace_hbm, tplace_ref),
-            (w1_hbm, w1_ref), (mf_hbm, mf_ref), (mw_hbm, mw_ref),
-        ])
-    ]
-    for copy in copies:
-        copy.start()
-    for copy in copies:
-        copy.wait()
-    own = rhs_ref.shape[1] // GS
-    c0 = scale_ref[:, 0:1]
-    c1 = scale_ref[:, 1:2]
-
-    def group(g, _):
-        at = pl.multiple_of(g * GS, GS)
-        w = w1_ref[:, pl.ds(at, GS)]
-        m = c0 * mf_ref[:, pl.ds(at, GS)] + c1 * mw_ref[:, pl.ds(at, GS)]
-        f = rhs_ref[:, pl.ds(at, GS)]
-        splace = splace_ref[:, pl.ds(pl.multiple_of(at + HALO * GS, GS), GS)]
-        tplace = tplace_ref[:, pl.ds(at, GS)]
-        slive = slot_mask(scnt_ref, g)
-        tlive = slot_mask(tcnt_ref, g)
-        for h in range(CHUNKS):
-            lanes = slice(h * LANES, (h + 1) * LANES)
-            coef = c0 * f[:, lanes] + c1 * gather(w, splace[:, lanes])
-            coef_ref[:, pl.ds(at + h * LANES, LANES)] = jnp.where(slive[:, lanes], coef, 0.0)
-            out = gather(m, tplace[:, lanes])
-            mapped_ref[:, pl.ds(at + h * LANES, LANES)] = jnp.where(tlive[:, lanes], out, 0.0)
+    scale = jnp.concatenate([c0, c1, jnp.zeros((LANES - 2, LANES), f32)], 0).T[:F]
+    c0 = scale[:, 0:1]
+    c1 = scale[:, 1:2]
+
+    def combine(g, _):
+        at = pl.ds(pl.multiple_of(g * GS, GS), GS)
+        coef_ref[:, at] = c0 * rhs_ref[:, at] + c1 * w1_ref[:, at]
+        mapped_ref[:, at] = c0 * mf_ref[:, at] + c1 * mw_ref[:, at]
         return 0
 
-    lax.fori_loop(0, own, group, 0)
+    lax.fori_loop(0, own, combine, 0)
 
 
 def run_local(scnt, tcnt, before, after, rhs, src, tgt):
@@ -525,7 +530,7 @@
             jax.ShapeDtypeStruct((F, points), f32),
             jax.ShapeDtypeStruct((8, LANES), f32),
         ],
-        in_specs=[smem, smem] + [vmem] * 5,
+        in_specs=[smem, smem] + [vmem] * 7,
         out_specs=[vmem] * 6,
         scratch_shapes=[
             pltpu.VMEM((16, total * GS), f32),
@@ -546,65 +551,94 @@
         ],
         compiler_params=pltpu.CompilerParams(vmem_limit_bytes=56 * 1024 * 1024),
         name="local",
-    )(scnt, tcnt, before, after, rhs, src, tgt)
-
-
-def run_share(sums, sizes):
-    vmem = pl.BlockSpec(memory_space=pltpu.VMEM)
-    return pl.pallas_call(
-        share_kernel,
-        out_shape=jax.ShapeDtypeStruct((F, LANES), f32),
-        in_specs=[vmem],
-        out_specs=vmem,
-        scratch_shapes=[
-            pltpu.VMEM((sizes[1], 8, LANES), f32),
-            pltpu.VMEM((sizes[0], 8, LANES), f32),
-            pltpu.SemaphoreType.DMA((sizes[1],)),
-            pltpu.SemaphoreType.DMA((sizes[1],)),
-            pltpu.SemaphoreType.DMA((sizes[0],)),
-            pltpu.SemaphoreType.DMA((sizes[0],)),
-        ],
-        compiler_params=pltpu.CompilerParams(collective_id=1, has_side_effects=True),
-        name="share",
-    )(sums)
-
-
-def run_final(scnt, tcnt, scale, *arrays):
+    )(scnt, tcnt, *before, *after, rhs, src, tgt)
+
+
+def run_finish(scnt, tcnt, sums, sizes, *arrays):
     vmem = pl.BlockSpec(memory_space=pltpu.VMEM)
     smem = pl.BlockSpec(memory_space=pltpu.SMEM)
     anywhere = pl.BlockSpec(memory_space=pl.ANY)
+    semaphores = [pltpu.SemaphoreType.DMA((n,)) for n in (len(arrays), sizes[1], sizes[1], sizes[0], sizes[0])]
     return pl.pallas_call(
-        final_kernel,
+        finish_kernel,
         out_shape=[jax.ShapeDtypeStruct(arrays[0].shape, f32)] * 2,
         in_specs=[smem, smem, vmem] + [anywhere] * len(arrays),
         out_specs=[vmem] * 2,
         scratch_shapes=[pltpu.VMEM(a.shape, a.dtype) for a in arrays]
-        + [pltpu.SemaphoreType.DMA((len(arrays),))],
-        compiler_params=pltpu.CompilerParams(vmem_limit_bytes=60 * 1024 * 1024),
-        name="final",
-    )(scnt, tcnt, scale, *arrays)
-
-
-def shifted(x, by):
-    peers = lax.axis_size(AXES)
-    pairs = [(i, i + by) for i in range(peers) if 0 <= i + by < peers]
-    return lax.ppermute(x, AXES, pairs)
+        + [pltpu.VMEM((sizes[1], 8, LANES), f32), pltpu.VMEM((sizes[0], 8, LANES), f32)]
+        + semaphores,
+        compiler_params=pltpu.CompilerParams(
+            vmem_limit_bytes=60 * 1024 * 1024, collective_id=1, has_side_effects=True
+        ),
+        name="finish",
+    )(scnt, tcnt, sums, *arrays)
+
+
+def halo_kernel(rhs, points, count, bf, bx, bc, af, ax, ac, send, recv):
+    reach = HALO * GS
+    me = [lax.axis_index(name) for name in AXES]
+    sizes = [lax.axis_size(name) for name in AXES]
+    peers = sizes[0] * sizes[1]
+    here = me[0] * sizes[1] + me[1]
+
+    def at(by):
+        place = lax.rem(here + by + peers, peers)
+        return (place // sizes[1], lax.rem(place, sizes[1]))
+
+    barrier = pltpu.get_barrier_semaphore()
+    for by in (1, -1):
+        pl.semaphore_signal(barrier, inc=1, device_id=at(by), device_id_type=pl.DeviceIdType.MESH)
+    pl.semaphore_wait(barrier, 2)
+    last = pl.ds(rhs.shape[1] - reach, reach)
+    first = pl.ds(0, reach)
+    copies = []
+    for by, moves in (
+        (1, ((rhs.at[:, last], bf), (points.at[:, last], bx), (count, bc))),
+        (-1, ((rhs.at[:, first], af), (points.at[:, first], ax), (count, ac))),
+    ):
+        for source, target in moves:
+            n = len(copies)
+            copy = pltpu.make_async_remote_copy(
+                src_ref=source, dst_ref=target, send_sem=send.at[n], recv_sem=recv.at[n],
+                device_id=at(by), device_id_type=pl.DeviceIdType.MESH,
+            )
+            copy.start()
+            copies.append(copy)
+    for copy in copies:
+        copy.wait()
+
+
+def run_halo(rhs, points, count):
+    reach = HALO * GS
+    anywhere = pl.BlockSpec(memory_space=pl.ANY)
+    side = [
+        jax.ShapeDtypeStruct((F, reach), f32),
+        jax.ShapeDtypeStruct((3, reach), f32),
+        jax.ShapeDtypeStruct(count.shape, i32),
+    ]
+    return pl.pallas_call(
+        halo_kernel,
+        out_shape=side * 2,
+        in_specs=[anywhere] * 3,
+        out_specs=[anywhere] * 6,
+        scratch_shapes=[pltpu.SemaphoreType.DMA((6,)), pltpu.SemaphoreType.DMA((6,))],
+        compiler_params=pltpu.CompilerParams(collective_id=2, has_side_effects=True),
+        name="halo",
+    )(rhs, points, count)
 
 
 def on_device(src_points, tgt_points, src_count, tgt_count, pair_list, pair_total, rhs):
-    reach = HALO * GS
     blocks = HALO * R
-    counts = src_count.astype(f32)
-    edges = [
-        jnp.concatenate([rhs[:, part], src_points[:, part], jnp.pad(counts[rows], (0, reach - blocks))[None]], 0)
-        for part, rows in ((slice(-reach, None), slice(-blocks, None)), (slice(0, reach), slice(0, blocks)))
-    ]
-    before = shifted(edges[0], 1)
-    after = shifted(edges[1], -1)
-    scnt = jnp.concatenate([before[11, :blocks].astype(i32), src_count, after[11, :blocks].astype(i32)])
-    splace, tplace, w1, mf, mw, sums = run_local(scnt, tgt_count, before, after, rhs, src_points, tgt_points)
-    scale = run_share(sums, [lax.axis_size(name) for name in AXES])
-    return run_final(src_count, tgt_count, scale, rhs, splace, tplace, w1, mf, mw)
+    bf, bx, bc, af, ax, ac = run_halo(rhs, src_points, src_count)
+    me = lax.axis_index(AXES)
+    bc = jnp.where(me > 0, bc[-blocks:], 0)
+    ac = jnp.where(me < lax.axis_size(AXES) - 1, ac[:blocks], 0)
+    scnt = jnp.concatenate([bc, src_count, ac])
+    splace, tplace, w1, mf, mw, sums = run_local(
+        scnt, tgt_count, (bf, bx), (af, ax), rhs, src_points, tgt_points
+    )
+    sizes = [lax.axis_size(name) for name in AXES]
+    return run_finish(src_count, tgt_count, sums, sizes, rhs, splace, tplace, w1, mf, mw)
 
 
 def solution(mesh):

time: 164 us -> 157 us (0.957)
  starting transfers between devices: 6.43 us -> 0 us
  local copies, waits for them, and re-layouts: 1.77 us -> 4.04 us
  waiting for transfers between devices: 1.91 us -> 0 us
    ppermute x2 -> x0, starting transfers between devices: 6.43 us -> none  [shifted(): return lax.ppermute(x, AXES, pairs)]
    unnamed x6 -> x10, local copies, waits for them, and re-layouts: 0.01 us -> 4.04 us
    pallas_call x2, Pallas kernels: 30.3 us -> 33.7 us  [the longest x1 22.8 us: run_finish(): pl.pallas_call(finish_kernel, out_shape=[jax.ShapeDtypeStruct(arrays[0].s...]
    pallas_call x1, Pallas kernels: 121 us -> 118 us  [run_local(): pl.pallas_call(local_kernel, out_shape=[jax.ShapeDtypeStruct((1, total *...]
    ppermute x2 -> x0, waiting for transfers between devices: 1.91 us -> none  [shifted(): return lax.ppermute(x, AXES, pairs)]
    slice x3 -> x0, local copies, waits for them, and re-layouts: 1.75 us -> none  [the longest x1 0.89 us: on_device(): rhs[:, part]]
  transfers between devices with their start and end apart: 2 -> 0, of which waited for: 2 -> 0; matrix products, arithmetic and copies ran while one was open for 0% -> 0% of each run, Pallas kernels for 0% -> 0%
where the time goes in v5:
time: 157 us
  Pallas kernels  152 us (97%)
  local copies, waits for them, and re-layouts  4.04 us (3%)
    pallas_call x1, Pallas kernels, run_local(): pl.pallas_call(local_kernel, out_shape=[jax.ShapeDtypeStruct((1, total *...  118 us
    pallas_call x1, Pallas kernels, run_finish(): pl.pallas_call(finish_kernel, out_shape=[jax.ShapeDtypeStruct(arrays[0].s...  22.8 us
    pallas_call x1, Pallas kernels, run_halo(): pl.pallas_call(halo_kernel, out_shape=side * 2, in_specs=[anywhere] * 3,...  10.9 us
    unnamed x10, local copies, waits for them, and re-layouts  4.04 us

profile of v5, /device:TPU:1, one launch (start us, length us, event | category | flops | bytes accessed | tf_op | source)
XLA Modules:
  0.0 157.2 jit_solution(13405941854295399898)
XLA Ops:
  0.6 10.9 %halo.1 = (f32[8,2048]{1,0:T(8,128)}, f32[3,2048]{1,0:T(4,128)}, s32[64]{0:T(128)}, f32[8,2048]{1,0:T(8,128)}, f32[3,2048]{1,0:T(4,128)}, /*index=5*/s32[64]{0:T(128)}) custom-call(f32[8,16384]{1,0:T(8,128)} %rhs_hbm.1, f32[3,16384]{1,0:T(4,128)} %points_ref.1, s32[64]{0:T(128)} %scnt_ref.1), custom_call_target="tpu_custom_call" | custom-call | tf_op jit(solution)/shard_map/halo/pallas_call | solution.py:619
  11.6 0.0 copy-start.2
  11.6 0.0 copy-start.3
  11.6 0.6 copy-done.2
  12.2 0.1 copy-done.3
  12.2 0.1 broadcast_select_fusion
  12.3 0.0 copy-start.1
  12.3 0.7 copy-done.1
  13.0 0.6 pad_add_fusion.scnt_ref
  13.6 118.1 %local.1 = (s32[1,20480]{1,0:T(1,128)}, s32[1,16384]{1,0:T(1,128)}, f32[8,16384]{1,0:T(8,128)}, f32[8,16384]{1,0:T(8,128)}, f32[8,16384]{1,0:T(8,128)}, /*index=5*/f32[8,128]{1,0:T(8,128)}) custom-call(s32[80]{0:T(128)} %pad_add_fusion.scnt_ref, s32[64]{0:T(128)} %tcnt_ref.3, f32[8,2048]{1,0:T(8,128)} %get-tuple-element.16.bf_ref, ...), custom_call_target="tpu_custom_call" | custom-call | tf_op jit(solution)/shard_map/local/pallas_call | solution.py:523
  131.7 22.8 %finish.1 = (f32[8,16384]{1,0:T(8,128)}, f32[8,16384]{1,0:T(8,128)}) custom-call(s32[64]{0:T(128)} %scnt_ref.1, s32[64]{0:T(128)} %tcnt_ref.3, f32[8,128]{1,0:T(8,128)} %get-tuple-element.20.sums_ref, f32[8,16384]{1,0:T(8,128)} %rhs_hbm.1, s32[1,20480]{1,0:T(1,128)} %get-tuple-element.21.splace_hbm, s32[1,16384]{1,0:T(1,128)} %get-tuple-element.22.tplace_hbm, ...), custom_call_target="tpu_custom_call" | custom-call | tf_op jit(solution)/shard_map/finish/pallas_call | solution.py:562
  154.4 0.0 copy-start
  154.4 1.9 %copy.9 = f32[8,16384]{1,0:T(8,128)} copy(f32[8,16384]{1,0:T(8,128)} %get-tuple-element.30) | data formatting | bytes 1048576
  156.4 0.0 copy-done
  156.4 0.8 copy.10
Async XLA Ops:
  11.6 0.6 copy-start.2
  11.6 0.7 copy-start.3
  12.3 0.7 copy-start.1
  154.4 1.9 %copy-start = (f32[8,16384]{1,0:T(8,128)S(1)}, f32[8,16384]{1,0:T(8,128)}, u32[]{:S(2)}) copy-start(f32[8,16384]{1,0:T(8,128)} %get-tuple-element.31) | copy-start | bytes 1572868

commit v6 on v5

--- a/solution.py
+++ b/solution.py
@@ -21,6 +21,7 @@
 VAL_STRIDE = GS + 384
 SEG = 256
 BATCH = 4
+MAPPED_BATCH = 8
 LAG = -(-15 // BATCH) + 1
 TOGETHER = 4
 AXES = ("src", "tgt")
@@ -221,11 +222,16 @@
             tlane_ref, pl.multiple_of(g * GS, GS), live_total(tcnt_ref, g), g + HALO, acc, g + total
         )
 
-    def two(fn, first):
-        return lambda i, acc: fn(first + 2 * i + 1, fn(first + 2 * i, acc))
-
-    acc = lax.fori_loop(0, (total - 2) // 2, two(source_windows, 1), jnp.zeros((8, LANES), i32))
-    wins_v[...] = lax.fori_loop(0, own // 2, two(target_windows, 0), acc)
+    def all_windows(fn, first, count, acc, together):
+        def some(i, acc):
+            for u in range(together):
+                acc = fn(first + together * i + u, acc)
+            return acc
+
+        return lax.fori_loop(0, count // together, some, acc)
+
+    acc = all_windows(source_windows, 1, total - 2, jnp.zeros((8, LANES), i32), 6)
+    wins_v[...] = all_windows(target_windows, 0, own, acc, 8)
     copy = pltpu.make_async_copy(wins_v, wins_s, sem)
     copy.start()
     copy.wait()
@@ -282,16 +288,16 @@
 
         return lax.fori_loop(first, end, list_group, 0)
 
-    def work_on(i, n, column0, g0, points_ref, cnt_ref, value_refs, place, keep=False, kept=False):
+    def work_on(i, n, column0, g0, points_ref, cnt_ref, value_refs, place, keep=False, kept=False, size=BATCH):
         work = []
-        for u in range(BATCH):
-            item = list_s[jnp.minimum(i * BATCH + u, n - 1)]
+        for u in range(size):
+            item = list_s[jnp.minimum(i * size + u, n - 1)]
             g = item // CHUNKS
             c = item % CHUNKS
             at = pl.multiple_of(item * LANES, LANES)
             packed = wins_s[c, g + column0]
             slot = lax.rem(i, LAG + 1) * BATCH + u
-            steps = jnp.where(i * BATCH + u < n, packed >> 21, 0)
+            steps = jnp.where(i * size + u < n, packed >> 21, 0)
             work.append((g, c, at, packed, points_ref[:, pl.ds(at, LANES)], slot, steps))
         accs = tuple(
             interact(
@@ -366,10 +372,14 @@
     n = list_chunks(tcnt_ref, 0, own)
 
     def mapped_pass(i, _):
-        run_rest(work_on(i, n, total, HALO, tlane_ref, tcnt_ref, [vf_ref, vw_ref], place_mapped))
+        run_rest(
+            work_on(
+                i, n, total, HALO, tlane_ref, tcnt_ref, [vf_ref, vw_ref], place_mapped, size=MAPPED_BATCH
+            )
+        )
         return 0
 
-    lax.fori_loop(0, (n + BATCH - 1) // BATCH, mapped_pass, 0)
+    lax.fori_loop(0, (n + MAPPED_BATCH - 1) // MAPPED_BATCH, mapped_pass, 0)
 
     def first_sums(g, acc):
         ff, fw = acc

time: 157 us -> 152 us (0.968)
  Pallas kernels: 152 us -> 147 us
    pallas_call x1, Pallas kernels: 118 us -> 111 us  [run_local(): pl.pallas_call(local_kernel, out_shape=[jax.ShapeDtypeStruct((1, total *...]
    pallas_call x1, Pallas kernels: 22.8 us -> 24.4 us  [run_finish(): pl.pallas_call(finish_kernel, out_shape=[jax.ShapeDtypeStruct(arrays[0].s...]
where the time goes in v6:
time: 152 us
  Pallas kernels  147 us (97%)
  local copies, waits for them, and re-layouts  4.04 us (3%)
    pallas_call x1, Pallas kernels, run_local(): pl.pallas_call(local_kernel, out_shape=[jax.ShapeDtypeStruct((1, total *...  111 us
    pallas_call x1, Pallas kernels, run_finish(): pl.pallas_call(finish_kernel, out_shape=[jax.ShapeDtypeStruct(arrays[0].s...  24.4 us
    pallas_call x1, Pallas kernels, run_halo(): pl.pallas_call(halo_kernel, out_shape=side * 2, in_specs=[anywhere] * 3,...  10.9 us
    unnamed x10, local copies, waits for them, and re-layouts  4.04 us

profile of v6, /device:TPU:1, one launch (start us, length us, event | category | flops | bytes accessed | tf_op | source)
XLA Modules:
  0.0 152.1 jit_solution(9301795472006417706)
XLA Ops:
  0.6 10.9 %halo.1 = (f32[8,2048]{1,0:T(8,128)}, f32[3,2048]{1,0:T(4,128)}, s32[64]{0:T(128)}, f32[8,2048]{1,0:T(8,128)}, f32[3,2048]{1,0:T(4,128)}, /*index=5*/s32[64]{0:T(128)}) custom-call(f32[8,16384]{1,0:T(8,128)} %rhs_hbm.1, f32[3,16384]{1,0:T(4,128)} %points_ref.1, s32[64]{0:T(128)} %scnt_ref.1), custom_call_target="tpu_custom_call" | custom-call | tf_op jit(solution)/shard_map/halo/pallas_call | solution.py:629
  11.6 0.0 copy-start.2
  11.6 0.0 copy-start.3
  11.6 0.6 copy-done.2
  12.2 0.1 copy-done.3
  12.2 0.1 broadcast_select_fusion
  12.3 0.0 copy-start.1
  12.3 0.7 copy-done.1
  13.0 0.6 pad_add_fusion.scnt_ref
  13.6 111.4 %local.1 = (s32[1,20480]{1,0:T(1,128)}, s32[1,16384]{1,0:T(1,128)}, f32[8,16384]{1,0:T(8,128)}, f32[8,16384]{1,0:T(8,128)}, f32[8,16384]{1,0:T(8,128)}, /*index=5*/f32[8,128]{1,0:T(8,128)}) custom-call(s32[80]{0:T(128)} %pad_add_fusion.scnt_ref, s32[64]{0:T(128)} %tcnt_ref.3, f32[8,2048]{1,0:T(8,128)} %get-tuple-element.16.bf_ref, ...), custom_call_target="tpu_custom_call" | custom-call | tf_op jit(solution)/shard_map/local/pallas_call | solution.py:533
  125.0 24.4 %finish.1 = (f32[8,16384]{1,0:T(8,128)}, f32[8,16384]{1,0:T(8,128)}) custom-call(s32[64]{0:T(128)} %scnt_ref.1, s32[64]{0:T(128)} %tcnt_ref.3, f32[8,128]{1,0:T(8,128)} %get-tuple-element.20.sums_ref, f32[8,16384]{1,0:T(8,128)} %rhs_hbm.1, s32[1,20480]{1,0:T(1,128)} %get-tuple-element.21.splace_hbm, s32[1,16384]{1,0:T(1,128)} %get-tuple-element.22.tplace_hbm, ...), custom_call_target="tpu_custom_call" | custom-call | tf_op jit(solution)/shard_map/finish/pallas_call | solution.py:572
  149.3 0.0 copy-start
  149.4 1.9 %copy.9 = f32[8,16384]{1,0:T(8,128)} copy(f32[8,16384]{1,0:T(8,128)} %get-tuple-element.30) | data formatting | bytes 1048576
  151.3 0.0 copy-done
  151.3 0.8 copy.10
Async XLA Ops:
  11.6 0.6 copy-start.2
  11.6 0.7 copy-start.3
  12.3 0.7 copy-start.1
  149.3 1.9 %copy-start = (f32[8,16384]{1,0:T(8,128)S(1)}, f32[8,16384]{1,0:T(8,128)}, u32[]{:S(2)}) copy-start(f32[8,16384]{1,0:T(8,128)} %get-tuple-element.31) | copy-start | bytes 1572868

commit v7 on v6

--- a/solution.py
+++ b/solution.py
@@ -122,10 +122,21 @@
 
 
 def local_kernel(
-    scnt_ref, tcnt_ref, bf_ref, bx_ref, af_ref, ax_ref, rhs_ref, points_ref, tgt_ref,
+    me_ref, bc_ref, cnt_ref, ac_ref, tcnt_ref, bf_ref, bx_ref, af_ref, ax_ref, rhs_ref, points_ref, tgt_ref,
     splace_ref, tplace_ref, w1_ref, mf_ref, mw_ref, sums_ref,
-    src_ref, rows_ref, vf_ref, vw_ref, lane_ref, tlane_ref, w2_ref, cache_ref, wins_v, wins_s, list_s, upper_ref, lower_ref, spread_ref, sem,
+    src_ref, rows_ref, vf_ref, vw_ref, lane_ref, tlane_ref, w2_ref, cache_ref, wins_v, wins_s, list_s, upper_ref, lower_ref, spread_ref, scnt_ref, sem,
 ):
+    blocks = HALO * R
+    inner = cnt_ref.shape[0]
+
+    def own_count(i, _):
+        scnt_ref[blocks + i] = cnt_ref[i]
+        return 0
+
+    lax.fori_loop(0, inner, own_count, 0)
+    for i in range(blocks):
+        scnt_ref[i] = jnp.where(me_ref[0] > 0, bc_ref[inner - blocks + i], 0)
+        scnt_ref[blocks + inner + i] = jnp.where(me_ref[0] < lax.axis_size(AXES) - 1, ac_ref[i], 0)
     own = tgt_ref.shape[1] // GS
     total = own + 2 * HALO
 
@@ -525,7 +536,7 @@
     lax.fori_loop(0, own, combine, 0)
 
 
-def run_local(scnt, tcnt, before, after, rhs, src, tgt):
+def run_local(me, bc, cnt, ac, tcnt, before, after, rhs, src, tgt):
     points = tgt.shape[1]
     total = points // GS + 2 * HALO
     vmem = pl.BlockSpec(memory_space=pltpu.VMEM)
@@ -540,7 +551,7 @@
             jax.ShapeDtypeStruct((F, points), f32),
             jax.ShapeDtypeStruct((8, LANES), f32),
         ],
-        in_specs=[smem, smem] + [vmem] * 7,
+        in_specs=[smem] * 5 + [vmem] * 7,
         out_specs=[vmem] * 6,
         scratch_shapes=[
             pltpu.VMEM((16, total * GS), f32),
@@ -557,11 +568,12 @@
             pltpu.VMEM((SEG, SEG), bf16),
             pltpu.VMEM((BINS, BINS), bf16),
             pltpu.VMEM((16, 3 * LANES), bf16),
+            pltpu.SMEM((total * R,), i32),
             pltpu.SemaphoreType.DMA,
         ],
         compiler_params=pltpu.CompilerParams(vmem_limit_bytes=56 * 1024 * 1024),
         name="local",
-    )(scnt, tcnt, *before, *after, rhs, src, tgt)
+    )(me, bc, cnt, ac, tcnt, *before, *after, rhs, src, tgt)
 
 
 def run_finish(scnt, tcnt, sums, sizes, *arrays):
@@ -638,14 +650,10 @@
 
 
 def on_device(src_points, tgt_points, src_count, tgt_count, pair_list, pair_total, rhs):
-    blocks = HALO * R
     bf, bx, bc, af, ax, ac = run_halo(rhs, src_points, src_count)
-    me = lax.axis_index(AXES)
-    bc = jnp.where(me > 0, bc[-blocks:], 0)
-    ac = jnp.where(me < lax.axis_size(AXES) - 1, ac[:blocks], 0)
-    scnt = jnp.concatenate([bc, src_count, ac])
+    me = lax.axis_index(AXES).astype(i32)[None]
     splace, tplace, w1, mf, mw, sums = run_local(
-        scnt, tgt_count, (bf, bx), (af, ax), rhs, src_points, tgt_points
+        me, bc, src_count, ac, tgt_count, (bf, bx), (af, ax), rhs, src_points, tgt_points
     )
     sizes = [lax.axis_size(name) for name in AXES]
     return run_finish(src_count, tgt_count, sums, sizes, rhs, splace, tplace, w1, mf, mw)

time: 152 us -> 152 us (level)
  Pallas kernels: 147 us -> 150 us
    pallas_call x1, Pallas kernels: 111 us -> 116 us  [run_local(): pl.pallas_call(local_kernel, out_shape=[jax.ShapeDtypeStruct((1, total *...]
    pallas_call x1, Pallas kernels: 24.4 us -> 22.2 us  [run_finish(): pl.pallas_call(finish_kernel, out_shape=[jax.ShapeDtypeStruct(arrays[0].s...]
    unnamed x10 -> x4, local copies, waits for them, and re-layouts: 4.04 us -> 2.72 us
where the time goes in v7:
time: 152 us; the launch traced here: 153 us
  Pallas kernels  150 us (99%)
  local copies, waits for them, and re-layouts  2.72 us (2%)
    pallas_call x1, Pallas kernels, run_local(): pl.pallas_call(local_kernel, out_shape=[jax.ShapeDtypeStruct((1, total *...  116 us
    pallas_call x1, Pallas kernels, run_finish(): pl.pallas_call(finish_kernel, out_shape=[jax.ShapeDtypeStruct(arrays[0].s...  22.2 us
    pallas_call x1, Pallas kernels, run_halo(): pl.pallas_call(halo_kernel, out_shape=side * 2, in_specs=[anywhere] * 3,...  10.9 us

profile of v7, /device:TPU:1, one launch (start us, length us, event | category | flops | bytes accessed | tf_op | source)
XLA Modules:
  0.0 152.9 jit_solution(10339727664092286423)
XLA Ops:
  0.6 10.9 %halo.1 = (f32[8,2048]{1,0:T(8,128)}, f32[3,2048]{1,0:T(4,128)}, s32[64]{0:T(128)}, f32[8,2048]{1,0:T(8,128)}, f32[3,2048]{1,0:T(4,128)}, /*index=5*/s32[64]{0:T(128)}) custom-call(f32[8,16384]{1,0:T(8,128)} %rhs_hbm.1, f32[3,16384]{1,0:T(4,128)} %points_ref.1, s32[64]{0:T(128)} %scnt_ref.1), custom_call_target="tpu_custom_call" | custom-call | tf_op jit(solution)/shard_map/halo/pallas_call | solution.py:641
  11.5 116.4 %local.1 = (s32[1,20480]{1,0:T(1,128)}, s32[1,16384]{1,0:T(1,128)}, f32[8,16384]{1,0:T(8,128)}, f32[8,16384]{1,0:T(8,128)}, f32[8,16384]{1,0:T(8,128)}, /*index=5*/f32[8,128]{1,0:T(8,128)}) custom-call(s32[1]{0:T(128)} %bitcast.me_ref, s32[64]{0:T(128)} %get-tuple-element.14.bc_ref, s32[64]{0:T(128)} %scnt_ref.1, s32[64]{0:T(128)} %get-tuple-element.15.ac_ref, ...), custom_call_target="tpu_custom_call" | custom-call | tf_op jit(solution)/shard_map/local/pallas_call | solution.py:544
  127.9 22.2 %finish.1 = (f32[8,16384]{1,0:T(8,128)}, f32[8,16384]{1,0:T(8,128)}) custom-call(s32[64]{0:T(128)} %scnt_ref.1, s32[64]{0:T(128)} %tcnt_ref.3, f32[8,128]{1,0:T(8,128)} %get-tuple-element.20.sums_ref, f32[8,16384]{1,0:T(8,128)} %rhs_hbm.1, s32[1,20480]{1,0:T(1,128)} %get-tuple-element.21.splace_hbm, s32[1,16384]{1,0:T(1,128)} %get-tuple-element.22.tplace_hbm, ...), custom_call_target="tpu_custom_call" | custom-call | tf_op jit(solution)/shard_map/finish/pallas_call | solution.py:584
  150.2 0.0 copy-start
  150.2 1.9 %copy.9 = f32[8,16384]{1,0:T(8,128)} copy(f32[8,16384]{1,0:T(8,128)} %get-tuple-element.28) | data formatting | bytes 1048576
  152.1 0.0 copy-done
  152.1 0.8 copy.10
Async XLA Ops:
  150.2 1.9 %copy-start = (f32[8,16384]{1,0:T(8,128)S(1)}, f32[8,16384]{1,0:T(8,128)}, u32[]{:S(2)}) copy-start(f32[8,16384]{1,0:T(8,128)} %get-tuple-element.29) | copy-start | bytes 1572868
